TPU v7x, 32 devices: a whole 2x2x4 slice. The times are simulated.
32 devices in a mesh: seq: 8 (over z, x), exp: 4 (over y, core).
Axes of the slice: x: 2, y: 2, z: 4, core: 2. Of those that a mesh axis runs over, the one named last changes fastest.
Arguments:
- mixer_input: bfloat16 [512, 8192], P('seq', 'exp'), may hold values from -6 to 6
- gate_input: bfloat16 [512, 8192], P('seq', 'exp'), may hold values from -6 to 6
- conv_weight: bfloat16 [4, 8192], P(None, 'exp'), may hold values from -3 to 3
- conv_bias: float32 [8192], P('exp'), may hold values from -3 to 3
- rank_weight: bfloat16 [8192, 256], P('exp'), may hold values from -0.0625 to 0.0625
- state_weight: bfloat16 [8192, 32], P('exp'), may hold values from -0.03125 to 0.03125
- delta_weight: bfloat16 [256, 8192], P(None, 'exp'), may hold values from -0.375 to 0.375
- delta_bias: float32 [8192], P('exp'), may hold values from -1 to 1
- log_rates: float32 [16, 8192], P(None, 'exp'), may hold values from -10 to -1
- skip_gain: float32 [8192], P('exp'), may hold values from 0.5 to 1.5
- out_proj: bfloat16 [8192, 4096], P('exp', 'seq'), may hold values from -0.0625 to 0.0625
- residual: bfloat16 [512, 4096], P(('seq', 'exp')), may hold values from -3 to 3
- norm_gain: float32 [4096], replicated, may hold values from 0.5 to 1.5
- router: float32 [4096, 4], replicated, may hold values from -0.09375 to 0.09375
- w_gate: bfloat16 [4, 4096, 14336], P('exp', None, 'seq'), may hold values from -0.09375 to 0.09375
- w_up: bfloat16 [4, 4096, 14336], P('exp', None, 'seq'), may hold values from -0.09375 to 0.09375
- w_down: bfloat16 [4, 14336, 4096], P('exp', 'seq'), may hold values from -0.09375 to 0.09375
- routes: int32 [512, 2], P(('seq', 'exp')), may hold values from 0 to 3, all different within a row; in each aligned block of 16 rows (0 to 15, 16 to 31, ...) at most 16 rows name the same one
Outputs:
- layer_out: bfloat16 [512, 4096], P(('seq', 'exp'))
- expert_mix: float32 [512, 4096], P(('seq', 'exp'))
Inputs may be any that keep to these rules, and one draw needn't show every extreme that they name: `routes`: each row names two different experts; among the 16 rows of one device no expert is named more than 16 times, a bound that some block reaches there on some device.
All inputs are finite; a program needn't handle non-finite values.
Results may differ from a plain program's by a relative error of at most 0.024.
Values may be sent and summed in bfloat16 or wider, within the bound.
A program may use at most 128 MiB of HBM per device.

v0:
```python
import jax
import jax.numpy as jnp
from jax import lax
from jax.sharding import PartitionSpec as P


def shifted(block, axis, distance):
    devices = range(lax.axis_size(axis))
    route = [(i - distance, i) for i in devices if i - distance in devices]
    return lax.ppermute(block, axis, route)


def entering(array, axis, combine, identity):
    count, index = (lax.axis_size(axis), lax.axis_index(axis))
    everything = jax.tree.map(lambda part: lax.all_gather(part, axis), array)
    start = jax.tree.map(
        lambda part, zero: jnp.broadcast_to(jnp.asarray(zero, part.dtype), part.shape),
        array,
        identity,
    )

    def hop(k, before):
        reached = k < index
        new = combine(before, jax.tree.map(lambda part: part[k], everything))
        return jax.tree.map(lambda a, b: jnp.where(reached, a, b), new, before)

    return lax.fori_loop(0, count, hop, start)


def combine_pair(earlier, following):
    return (earlier[0] * following[0], following[0] * earlier[1] + following[1])


def body(
    mixer_input,
    gate_input,
    conv_weight,
    conv_bias,
    rank_weight,
    state_weight,
    delta_weight,
    delta_bias,
    log_rates,
    skip_gain,
    out_proj,
    residual,
    norm_gain,
    router,
    w_gate,
    w_up,
    w_down,
    routes,
):
    taps = conv_weight.shape[0]
    block_rows = mixer_input.shape[0]
    rim_rows = shifted(mixer_input[block_rows - (taps - 1) :], "seq", 1)
    padded = jnp.concatenate([rim_rows, mixer_input], axis=0)
    conv_sum = jnp.zeros(mixer_input.shape, jnp.float32) + conv_bias[None, :]
    for offset in range(taps):
        conv_sum = conv_sum + conv_weight[offset].astype(jnp.float32)[None, :] * padded[
            offset : offset + block_rows
        ].astype(jnp.float32)
    conv_act = jax.nn.silu(conv_sum).astype(jnp.bfloat16)
    delta_part = jnp.dot(conv_act, rank_weight, preferred_element_type=jnp.float32)
    state_part = jnp.dot(conv_act, state_weight, preferred_element_type=jnp.float32)
    delta_sum, state_maps = lax.psum((delta_part, state_part), "exp")
    delta_low = delta_sum.astype(jnp.bfloat16)
    states = log_rates.shape[0]
    input_map = state_maps[:, :states]
    output_map = state_maps[:, states:]
    delta = jax.nn.softplus(
        jnp.dot(delta_low, delta_weight, preferred_element_type=jnp.float32) + delta_bias[None, :]
    )
    decay_rate = jnp.exp(log_rates)
    conv_float = conv_act.astype(jnp.float32)
    driven = (delta * conv_float)[:, None, :] * input_map[:, :, None]
    decays = jnp.exp(-delta[:, None, :] * decay_rate[None])
    passed = jnp.cumsum(delta, axis=0)
    total_dt = passed[-1]
    weights_left = jnp.exp(-(total_dt[None, :] - passed)[:, None, :] * decay_rate[None])
    transform = (jnp.exp(-total_dt[None, :] * decay_rate), jnp.sum(weights_left * driven, axis=0))
    incoming = entering(
        transform, "seq", combine_pair, (jnp.ones_like(decay_rate), jnp.zeros_like(decay_rate))
    )
    start_state = incoming[1]

    def advance(carried, inputs):
        decay_t, driven_t, output_t = inputs
        carried = decay_t * carried + driven_t
        return (carried, jnp.sum(output_t[:, None] * carried, axis=0))

    last_state, scan_out = lax.scan(advance, start_state, (decays, driven, output_map))
    scan_out = scan_out + skip_gain[None, :] * conv_float
    gated = (scan_out * jax.nn.silu(gate_input.astype(jnp.float32))).astype(jnp.bfloat16)
    tok_dev = residual.shape[0]
    partial_value = jnp.dot(
        gated,
        lax.all_gather(out_proj, "seq", axis=1, tiled=True),
        preferred_element_type=jnp.float32,
    )
    mamba_out = lax.psum_scatter(partial_value, "exp", scatter_dimension=0, tiled=True)
    hidden = residual.astype(jnp.float32) + mamba_out
    mean_square = jnp.mean(hidden * hidden, axis=1, keepdims=True)
    normed = (hidden * lax.rsqrt(mean_square + 1e-05) * norm_gain[None, :]).astype(jnp.bfloat16)
    logits = jnp.dot(normed.astype(jnp.float32), router, precision=lax.Precision.HIGHEST)
    experts = router.shape[1]
    expert_ids = jnp.arange(experts, dtype=jnp.int32)
    matches = (routes[:, :, None] == expert_ids[None, None, :]).astype(jnp.float32)
    chosen = jnp.sum(matches * logits[:, None, :], axis=2)
    route_weights = jax.nn.sigmoid(chosen - chosen[:, ::-1])
    capacity = max(2, 4 * tok_dev // experts)
    flat_ids = routes.reshape(-1)
    route_pos = jnp.arange(flat_ids.shape[0], dtype=jnp.int32)
    earlier_same = (flat_ids[:, None] == flat_ids[None, :]) & (
        route_pos[None, :] < route_pos[:, None]
    )
    slot_rank = jnp.sum(earlier_same.astype(jnp.int32), axis=1)
    slot_of = flat_ids * capacity + slot_rank
    slot_ids = jnp.arange(experts * capacity, dtype=jnp.int32)
    placing = (slot_ids[:, None] == slot_of[None, :]).astype(jnp.bfloat16)
    repeated = jnp.repeat(normed, 2, axis=0)
    outbound = jnp.dot(placing, repeated, preferred_element_type=jnp.float32).astype(jnp.bfloat16)
    arrived = lax.all_to_all(outbound, "exp", split_axis=0, concat_axis=0, tiled=True)
    gate_local = w_gate[0]
    up_local = w_up[0]
    down_local = w_down[0]
    shard_part = lax.all_gather(arrived, "seq", axis=0, tiled=True)
    gate_part = jnp.dot(shard_part, gate_local, preferred_element_type=jnp.float32)
    up_part = jnp.dot(shard_part, up_local, preferred_element_type=jnp.float32)
    activated = (jax.nn.silu(gate_part) * up_part).astype(jnp.bfloat16)
    expert_out = lax.psum_scatter(
        jnp.dot(activated, down_local, preferred_element_type=jnp.float32).astype(jnp.bfloat16),
        "seq",
        scatter_dimension=0,
        tiled=True,
    ).astype(jnp.float32)
    returned = lax.all_to_all(expert_out, "exp", split_axis=0, concat_axis=0, tiled=True)
    picked = jnp.take(returned, slot_of, axis=0)
    moe_sum = jnp.sum(picked.reshape(tok_dev, 2, -1) * route_weights[:, :, None], axis=1)
    return ((hidden + moe_sum).astype(jnp.bfloat16), moe_sum)


def solution(mesh):
    in_specs = (
        P("seq", "exp"),
        P("seq", "exp"),
        P(None, "exp"),
        P("exp"),
        P("exp", None),
        P("exp", None),
        P(None, "exp"),
        P("exp"),
        P(None, "exp"),
        P("exp"),
        P("exp", "seq"),
        P(("seq", "exp"), None),
        P(),
        P(),
        P("exp", None, "seq"),
        P("exp", None, "seq"),
        P("exp", "seq", None),
        P(("seq", "exp"), None),
    )
    out_specs = (P(("seq", "exp"), None), P(("seq", "exp"), None))
    return jax.shard_map(body, mesh=mesh, in_specs=in_specs, out_specs=out_specs, check_vma=False)
```

profile of v0, /device:TPU:0, one launch (start us, length us, event | category | flops | bytes accessed | tf_op | source)
XLA Modules:
  0.0 634.6 jit_solution(8615766575032266392)
XLA Ops:
  8.1 4.8 collective-permute-start
  14.4 1.9 multiply_convert_fusion.1
  16.2 1.5 fusion.38
  18.8 11.1 %all-reduce = (bf16[64,256]{1,0:T(8,128)(2,1)S(1)}, f32[64,32]{0,1:T(8,128)S(1)}) all-reduce(f32[64,256]{1,0:T(8,128)S(1)} %fusion.38, f32[64,32]{0,1:T(8,128)S(1)} %fusion.39), channel_id=1, replica_groups=mesh['seq'=8,'exp'=4] {'exp'}, use_global_device_ids=true, to_apply=%region_0.1 | all-reduce | flops 18432 | bytes 114688 | tf_op jit(solution)/shard_map/psum | solution.py:66
  29.9 1.2 fusion.34
  31.8 1.6 fusion.36
  33.4 7.9 %broadcast_multiply_fusion = (f32[64,16,2048]{2,1,0:T(8,128)}, f32[16,2048]{1,0:T(8,128)}, f32[64,16,2048]{2,1,0:T(8,128)}) fusion(f32[64,16]{1,0:T(8,128)S(1)} %copy.37, f32[64,2048]{1,0:T(8,128)S(1)} %get-tuple-element.201, f32[16,2048]{1,0:T(8,128)S(1)} %get-tuple-element.205, f32[64,2048]{1,0:T(8,128)S(1)} %subtract_negate_fusion, ...), kind=kLoop, calls=%fused_computation.19 | loop fusion | flops 10452992 | bytes 18616320 | tf_op jit(solution)/shard_map/mul | solution.py:76
  43.0 40.9 %all-gather.13.cloned.1.call-done = f32[128,2048]{1,0:T(8,128)} async-done(((f32[16,2048]{1,0:T(8,128)}), f32[128,2048]{1,0:T(8,128)}) %all-gather.13.cloned.1.call-update) | async-done | bytes 1048592 | tf_op jit(solution)/shard_map/all_gather | solution.py:15
  83.9 41.6 %all-gather.11.cloned.1.call-done = f32[128,2048]{1,0:T(8,128)} async-done(((f32[16,2048]{1,0:T(8,128)}), f32[128,2048]{1,0:T(8,128)}) %all-gather.11.cloned.1.call-update) | async-done | bytes 1048592 | tf_op jit(solution)/shard_map/all_gather | solution.py:15
  125.5 8.8 %while.29 = (s32[]{:T(128)}, f32[16,2048]{1,0:T(8,128)S(1)}, s32[]{:T(128)}, f32[8,16,2048]{2,1,0:T(8,128)}, f32[8,16,2048]{2,1,0:T(8,128)}) while((s32[]{:T(128)}, f32[16,2048]{1,0:T(8,128)S(1)}, s32[]{:T(128)}, f32[8,16,2048]{2,1,0:T(8,128)}, f32[8,16,2048]{2,1,0:T(8,128)}) %tuple.92), condition=%wide.region_5.6_spmd.clone.clone, body=%wide.region_4.5_spmd.clone.sunk.clone | while | flops 131076 | bytes 524373 | solution.py:27
  134.3 85.6 %while.28 = (s32[]{:T(128)}, f32[16,2048]{1,0:T(8,128)S(1)}, f32[64,2048]{1,0:T(8,128)S(1)}, f32[64,16,2048]{2,1,0:T(8,128)}, f32[64,16,2048]{2,1,0:T(8,128)}, /*index=5*/f32[64,16]{1,0:T(8,128)S(1)}) while((s32[]{:T(128)}, f32[16,2048]{1,0:T(8,128)S(1)}, f32[64,2048]{1,0:T(8,128)S(1)}, f32[64,16,2048]{2,1,0:T(8,128)}, ...), condition=%wide.region_8.9_spmd.clone, body=%wide.region_6.8_spmd.sunk.clone | while | flops 129026 | bytes 549137 | solution.py:92
  134.3 1.2 multiply_reduce_fusion.6
  135.8 1.2 multiply_reduce_fusion.6
  219.9 134.2 %all-gather.7.cloned.1.call-done = bf16[2048,4096]{1,0:T(8,128)(2,1)} async-done(((bf16[2048,512]{1,0:T(8,128)(2,1)}), bf16[2048,4096]{1,0:T(8,128)(2,1)}) %all-gather.7.cloned.1.call-update) | async-done | bytes 16777232 | tf_op jit(solution)/shard_map/all_gather | solution.py:98
  354.1 9.8 %fusion.24 = f32[64,4096]{1,0:T(8,128)} fusion(bf16[2048,4096]{1,0:T(8,128)(2,1)} %all-gather.7.cloned.1.call-done, f32[64,2048]{1,0:T(8,128)S(1)} %get-tuple-element.129, bf16[64,2048]{1,0:T(8,128)(2,1)S(1)} %multiply_convert_fusion.1, bf16[64,2048]{1,0:T(8,128)(2,1)S(1)} %copy-done.5, f32[2048]{0:T(1024)S(1)} %copy-done.6), kind=kOutput, calls=%fused_computation.43 | convolution fusion | flops 1075052544 | bytes 18882560 | tf_op jit(solution)/shard_map/dot_general | solution.py:96
  364.4 22.9 %reduce-scatter.3.cloned.1.call-done = f32[16,4096]{1,0:T(8,128)} async-done(((f32[64,4096]{1,0:T(8,128)}), f32[16,4096]{1,0:T(8,128)}) %reduce-scatter.3.cloned.1.call-update) | async-done | bytes 262160 | tf_op jit(solution)/shard_map/reduce_scatter | solution.py:101
  390.0 11.9 %all_to_all.28 = bf16[4,16,4096]{2,1,0:T(8,128)(2,1)} all-to-all(bf16[4,16,4096]{2,1,0:T(8,128)(2,1)S(1)} %bitcast.79), channel_id=1, replica_groups=mesh['seq'=8,'exp'=4] {'exp'}, dimensions={0} | all-to-all | bytes 1048576 | tf_op jit(solution)/shard_map/all_to_all | solution.py:123
  402.2 73.3 %all-gather.9.cloned.1.call-done = bf16[512,4096]{1,0:T(8,128)(2,1)} async-done(((bf16[64,4096]{1,0:T(8,128)(2,1)}), bf16[512,4096]{1,0:T(8,128)(2,1)}) %all-gather.9.cloned.1.call-update) | async-done | bytes 4194320 | tf_op jit(solution)/shard_map/all_gather | solution.py:127
  475.5 14.6 %fusion.6 = f32[512,1792]{1,0:T(8,128)} fusion(bf16[512,4096]{1,0:T(8,128)(2,1)} %all-gather.9.cloned.1.call-done, bf16[1,4096,1792]{2,1,0:T(8,128)(2,1)} %param.36), kind=kOutput, calls=%fused_computation.13 | convolution fusion | flops 7516192768 | bytes 22544384 | tf_op jit(solution)/shard_map/dot_general | solution.py:128
  490.1 28.7 %fusion.8 = bf16[512,4096]{1,0:T(8,128)(2,1)} fusion(bf16[1,1792,4096]{2,1,0:T(8,128)(2,1)} %param.38, f32[512,1792]{1,0:T(8,128)} %fusion.6, bf16[512,4096]{1,0:T(8,128)(2,1)} %all-gather.9.cloned.1.call-done, bf16[1,4096,1792]{2,1,0:T(8,128)(2,1)} %param.37), kind=kOutput, calls=%fused_computation.17 | convolution fusion | flops 15039987712 | bytes 41418752 | tf_op jit(solution)/shard_map/dot_general | solution.py:132
  519.2 86.0 %reduce-scatter.5.cloned.1.call-done = bf16[64,4096]{1,0:T(8,128)(2,1)} async-done(((bf16[512,4096]{1,0:T(8,128)(2,1)}), bf16[64,4096]{1,0:T(8,128)(2,1)}) %reduce-scatter.5.cloned.1.call-update) | async-done | bytes 524304 | tf_op jit(solution)/shard_map/reduce_scatter | solution.py:131
  605.2 2.1 convert.5
  607.2 3.5 all-to-all-start.1
  611.3 13.9 %all-to-all-done.1 = f32[4,16,4096]{2,1,0:T(8,128)S(1)} async-done(((f32[4,16,4096]{2,1,0:T(8,128)}), f32[4,16,4096]{2,1,0:T(8,128)S(1)}, u32[]{:S(2)}, u32[]{:S(2)}) %all-to-all-start.1) | async-done | bytes 1048608 | tf_op jit(solution)/shard_map/all_to_all | solution.py:137
  (270 shorter events, 102.2 us)
Async XLA Ops:
  7.2 22.7 %copy-start = (bf16[256,2048]{1,0:T(8,128)(2,1)S(1)}, bf16[256,2048]{1,0:T(8,128)(2,1)}, u32[]{:S(2)}) copy-start(bf16[256,2048]{1,0:T(8,128)(2,1)} %param.28) | copy-start | bytes 3145732
  7.2 76.7 %all-gather.13.cloned.1.call-start = ((), (), s32[]{:S(2)}) async-start(), calls=%async_computation.9 | async-start | bytes 1179648 | tf_op jit(solution)/shard_map/all_gather | solution.py:15
  8.1 6.3 collective-permute-start
  33.4 320.7 %copy-start.5 = (bf16[64,2048]{1,0:T(8,128)(2,1)S(1)}, bf16[64,2048]{1,0:T(8,128)(2,1)}, u32[]{:S(2)}) copy-start(bf16[64,2048]{1,0:T(8,128)(2,1)} %param.23) | copy-start | bytes 786436
  33.4 320.7 %copy-start.6 = (f32[2048]{0:T(1024)S(1)}, f32[2048]{0:T(1024)}, u32[]{:S(2)}) copy-start(f32[2048]{0:T(1024)} %param.31) | copy-start | bytes 24580
  41.4 84.2 %all-gather.11.cloned.1.call-start = ((), (), s32[]{:S(2)}) async-start(), calls=%async_computation.8 | async-start | bytes 1179648 | tf_op jit(solution)/shard_map/all_gather | solution.py:15
  42.1 312.0 %all-gather.7.cloned.1.call-start = ((), (), s32[]{:S(2)}) async-start(), calls=%async_computation.4 | async-start | bytes 18874368 | tf_op jit(solution)/shard_map/all_gather | solution.py:98
  42.8 344.4 %reduce-scatter.3.cloned.1.call-start = ((), (), s32[]{:S(2)}) async-start(), calls=%async_computation.5 | async-start | bytes 1310720 | tf_op jit(solution)/shard_map/reduce_scatter | solution.py:101
  354.1 9.9 %copy-start.9 = (s32[16,2]{0,1:T(2,128)S(1)}, s32[16,2]{0,1:T(2,128)}, u32[]{:S(2)}) copy-start(s32[16,2]{0,1:T(2,128)} %param.39) | copy-start | bytes 388
  354.1 33.1 %copy-start.3 = (bf16[16,4096]{1,0:T(8,128)(2,1)S(1)}, bf16[16,4096]{1,0:T(8,128)(2,1)}, u32[]{:S(2)}) copy-start(bf16[16,4096]{1,0:T(8,128)(2,1)} %param.33) | copy-start | bytes 393220
  354.1 34.2 %copy-start.8 = (f32[4096]{0:T(1024)S(1)}, f32[4096]{0:T(1024)}, u32[]{:S(2)}) copy-start(f32[4096]{0:T(1024)} %param.34) | copy-start | bytes 49156
  364.0 111.5 %all-gather.9.cloned.1.call-start = ((), (), s32[]{:S(2)}) async-start(), calls=%async_computation.6 | async-start | bytes 4718592 | tf_op jit(solution)/shard_map/all_gather | solution.py:127
  402.0 203.2 %reduce-scatter.5.cloned.1.call-start = ((), (), s32[]{:S(2)}) async-start(), calls=%async_computation.7 | async-start | bytes 4718592 | tf_op jit(solution)/shard_map/reduce_scatter | solution.py:131
  490.1 120.8 %copy-start.7 = (f32[4096,4]{0,1:T(4,128)S(1)}, f32[4096,4]{0,1:T(4,128)}, u32[]{:S(2)}) copy-start(f32[4096,4]{0,1:T(4,128)} %param.35) | copy-start | bytes 196612
  490.1 137.7 %copy-start.1 = (bf16[256,2048]{1,0:T(8,128)(2,1)S(1)}, bf16[256,2048]{1,0:T(8,128)(2,1)}, u32[]{:S(2)}) copy-start(bf16[256,2048]{1,0:T(8,128)(2,1)} %param.28) | copy-start | bytes 3145732
  518.8 108.2 %copy-start.2 = (f32[16,4096]{1,0:T(8,128)S(1)}, f32[16,4096]{1,0:T(8,128)}, u32[]{:S(2)}) copy-start(f32[16,4096]{1,0:T(8,128)} %reduce-scatter.3.cloned.1.call-done) | copy-start | bytes 786436
  607.2 18.0 %all-to-all-start.1 = ((f32[4,16,4096]{2,1,0:T(8,128)}), f32[4,16,4096]{2,1,0:T(8,128)S(1)}, u32[]{:S(2)}, u32[]{:S(2)}) async-start(f32[4,16,4096]{2,1,0:T(8,128)} %convert.5), calls=%async_computation.3 | async-start | bytes 2097152 | tf_op jit(solution)/shard_map/all_to_all | solution.py:137
  627.0 0.7 copy-start.4
Sparse Core Ops, SparseCore 0:
  41.5 42.3 all-gather.12
  86.6 38.8 all-gather.10
  127.6 226.4 all-gather.6
  364.1 23.1 reduce-scatter.2
  402.1 73.3 all-gather.8
  519.0 86.1 reduce-scatter.4
where the time goes:
time: 637 us; the launch traced here: 635 us
  waiting for transfers between devices  415 us (65%)
  other arithmetic  97.2 us (15%)
  matrix products  57.5 us (9%)
  blocking collectives  23 us (4%)
  local copies, waits for them, and re-layouts  16.8 us (3%)
  between operations  14.4 us (2%)
  starting transfers between devices  8.78 us (1%)
    all_gather x1, waiting for transfers between devices, body(): lax.all_gather(out_proj, 'seq', axis=1, tiled=True)  134 us
    reduce_scatter x1, waiting for transfers between devices, body(): lax.psum_scatter(jnp.dot(activated, down_local, preferred_element_type=jn...  86 us
    all_gather x2, waiting for transfers between devices, entering(): everything = jax.tree.map(lambda part: lax.all_gather(part, axis), array)  82.5 us
    all_gather x1, waiting for transfers between devices, body(): shard_part = lax.all_gather(arrived, 'seq', axis=0, tiled=True)  73.3 us
    reduce_sum x64, other arithmetic, advance(): return (carried, jnp.sum(output_t[:, None] * carried, axis=0))  69.7 us
    dot_general x1, matrix products, body(): jnp.dot(activated, down_local, preferred_element_type=jnp.float32)  28.7 us
    reduce_scatter x1, waiting for transfers between devices, body(): lax.psum_scatter(partial_value, 'exp', scatter_dimension=0, tiled=True)  22.9 us
    dot_general x1, matrix products, body(): jnp.dot(shard_part, gate_local, preferred_element_type=jnp.float32)  14.6 us
  transfers between devices with their start and end apart: 8, of which 8 were waited for; matrix products, arithmetic and copies ran while one was open for 15% of the time, Pallas kernels for 0%

commit v1 on v0

v1 whole, which is shorter than its diff:
```python
import functools

import jax
import jax.numpy as jnp
from jax import lax
from jax.experimental import pallas as pl
from jax.experimental.pallas import tpu as pltpu
from jax.sharding import PartitionSpec as P

MESH = pl.DeviceIdType.MESH
BF16 = jnp.bfloat16
F32 = jnp.float32
VMEM_BYTES = 58 * 1024 * 1024
ORDER = "zxyc"


def axis_sizes(seq, exp):
    x = 1
    while 4 * x * x <= seq and seq % (2 * x) == 0:
        x *= 2
    c = 2 if exp % 2 == 0 else 1
    return {"z": seq // x, "x": x, "y": exp // c, "c": c}


def own_place(size):
    seq, exp = lax.axis_index("seq"), lax.axis_index("exp")
    return {"z": seq // size["x"], "x": seq % size["x"], "y": exp // size["c"], "c": exp % size["c"]}


def device_at(place, size):
    return (place["z"] * size["x"] + place["x"], place["y"] * size["c"] + place["c"])


def moved(place, size, axis, distance):
    return {**place, axis: (place[axis] + distance) % size[axis]}


def greet(size, axes):
    me = own_place(size)
    barrier = pltpu.get_barrier_semaphore()
    count = 0
    for axis in axes:
        for d in range(1, size[axis]):
            pl.semaphore_signal(
                barrier, inc=1, device_id=device_at(moved(me, size, axis, d), size), device_id_type=MESH
            )
            count += 1
    pl.semaphore_wait(barrier, count)


def held_after(size, axes):
    held = [()]
    for axis in axes:
        held = [h + (d,) for h in held for d in range(size[axis])]
    return held


def gather_kernel(size, flows, x_ref, out_ref, send_sem, recv_sem, own_sem):
    me = own_place(size)
    axes = [a for a in ORDER if a in flows[0][0]]
    greet(size, axes)

    def slot(offsets, path):
        place = dict(me)
        for axis, d in zip(path, offsets):
            place[axis] = (me[axis] + d) % size[axis]
        return tuple(place[a] for a in axes)

    own = pltpu.make_async_copy(x_ref, out_ref.at[slot((), ())], own_sem)
    own.start()
    sends, arrived, number = [], set(), {}
    for f, (path, _, _) in enumerate(flows):
        for offsets in held_after(size, path):
            number[(f, offsets)] = len(number)

    def window(ref, lo, hi):
        return ref.at[:, lo:hi]

    def arrive(f, offsets):
        path, lo, hi = flows[f]
        full = offsets + (0,) * (len(path) - len(offsets))
        if any(full) and (f, full) not in arrived:
            arrived.add((f, full))
            landing = window(out_ref.at[slot(full, path)], lo, hi)
            pltpu.make_async_copy(landing, landing, recv_sem.at[number[(f, full)]]).wait()

    for stage in range(len(flows[0][0])):
        for offsets in held_after(size, flows[0][0][:stage]):
            pass
        lists = [held_after(size, path[:stage]) for path, _, _ in flows]
        for k in range(max(len(held) for held in lists)):
            for f, (path, lo, hi) in enumerate(flows):
                if k >= len(lists[f]):
                    continue
                offsets = lists[f][k]
                arrive(f, offsets)
                axis = path[stage]
                for d in range(1, size[axis]):
                    here = slot(offsets, path)
                    source = x_ref if not any(offsets) else out_ref.at[here]
                    lands = offsets + ((size[axis] - d),) + (0,) * (len(path) - stage - 1)
                    copy = pltpu.make_async_remote_copy(
                        src_ref=window(source, lo, hi),
                        dst_ref=window(out_ref.at[here], lo, hi),
                        send_sem=send_sem.at[len(sends)],
                        recv_sem=recv_sem.at[number[(f, lands)]],
                        device_id=device_at(moved(me, size, axis, d), size),
                        device_id_type=MESH,
                    )
                    copy.start()
                    sends.append(copy)
    for f, (path, _, _) in enumerate(flows):
        for offsets in held_after(size, path):
            arrive(f, offsets)
    for copy in sends:
        copy.wait_send()
    own.wait()


def gather(block, size, paths, splits, collective_id):
    axes = [a for a in ORDER if a in paths[0]]
    edges = (0,) + tuple(splits) + (block.shape[1],)
    flows = [(tuple(p), lo, hi) for p, lo, hi in zip(paths, edges[:-1], edges[1:])]
    slots = len(flows)
    for a in axes:
        slots *= size[a]
    return pl.pallas_call(
        functools.partial(gather_kernel, size, flows),
        out_shape=jax.ShapeDtypeStruct(tuple(size[a] for a in axes) + block.shape, block.dtype),
        in_specs=[pl.BlockSpec(memory_space=pl.ANY)],
        out_specs=pl.BlockSpec(memory_space=pl.ANY),
        scratch_shapes=[
            pltpu.SemaphoreType.DMA((slots,)),
            pltpu.SemaphoreType.DMA((slots,)),
            pltpu.SemaphoreType.DMA,
        ],
        compiler_params=pltpu.CompilerParams(
            collective_id=collective_id, has_side_effects=True, vmem_limit_bytes=VMEM_BYTES
        ),
        name="gather_" + "".join(axes),
    )(block)


def channels_kernel(size, part_ref, out_ref, landed, summed, spread, send_sem, recv_sem, send2, recv2):
    seq, exp = size["z"] * size["x"], size["y"] * size["c"]
    s, e = lax.axis_index("seq"), lax.axis_index("exp")
    barrier = pltpu.get_barrier_semaphore()
    for d in range(1, exp):
        pl.semaphore_signal(barrier, inc=1, device_id=(s, (e + d) % exp), device_id_type=MESH)
    for d in range(1, seq):
        pl.semaphore_signal(barrier, inc=1, device_id=((s + d) % seq, e), device_id_type=MESH)
    pl.semaphore_wait(barrier, exp + seq - 2)
    copies = []
    for d in range(1, exp):
        to = (e + d) % exp
        copy = pltpu.make_async_remote_copy(
            src_ref=part_ref.at[to],
            dst_ref=landed.at[exp - d - 1],
            send_sem=send_sem.at[d - 1],
            recv_sem=recv_sem.at[exp - d - 1],
            device_id=(s, to),
            device_id_type=MESH,
        )
        copy.start()
        copies.append(copy)
    for copy in copies:
        copy.wait()

    def add(k, carry):
        total = part_ref[e, k].astype(F32)
        for d in range(exp - 1):
            total = total + landed[d, k].astype(F32)
        summed[k] = total.astype(BF16)
        return carry

    lax.fori_loop(0, seq, add, 0)
    copies = []
    for d in range(1, seq):
        to = (s + d) % seq
        copy = pltpu.make_async_remote_copy(
            src_ref=summed.at[to],
            dst_ref=spread.at[s],
            send_sem=send2.at[d - 1],
            recv_sem=recv2.at[seq - d - 1],
            device_id=(to, e),
            device_id_type=MESH,
        )
        copy.start()
        copies.append(copy)
    for copy in copies:
        copy.wait_send()
    for d in range(1, seq):
        block = spread.at[(s + d) % seq]
        pltpu.make_async_copy(block, block, recv2.at[d - 1]).wait()
    spread[s] = summed[s]
    width = spread.shape[2]
    for k in range(seq):
        out_ref[:, k * width : (k + 1) * width] = spread[k].astype(F32)


def sum_channels(part, size, collective_id):
    exp, seq, rows, width = part.shape
    return pl.pallas_call(
        functools.partial(channels_kernel, size),
        out_shape=jax.ShapeDtypeStruct((rows, seq * width), F32),
        in_specs=[pl.BlockSpec(memory_space=pltpu.VMEM)],
        out_specs=pl.BlockSpec(memory_space=pltpu.VMEM),
        scratch_shapes=[
            pltpu.VMEM((exp - 1, seq, rows, width), BF16),
            pltpu.VMEM((seq, rows, width), BF16),
            pltpu.VMEM((seq, rows, width), BF16),
            pltpu.SemaphoreType.DMA((exp - 1,)),
            pltpu.SemaphoreType.DMA((exp - 1,)),
            pltpu.SemaphoreType.DMA((seq - 1,)),
            pltpu.SemaphoreType.DMA((seq - 1,)),
        ],
        compiler_params=pltpu.CompilerParams(
            collective_id=collective_id, has_side_effects=True, vmem_limit_bytes=VMEM_BYTES
        ),
        name="sum_channels",
    )(part)


def experts_kernel(size, part_ref, out_ref, *scratch):
    me = own_place(size)
    greet(size, "zxyc")
    half = part_ref.shape[-1] // 2
    rows = part_ref.shape[-2]
    from_core, first_a, first_b, land_a, land_b, second_a, second_b, land2_a, land2_b = scratch[:9]
    third_a, third_b, land3_a, land3_b, core_sems, sems = scratch[9:]
    cores = size["c"]
    pending = []
    if cores == 2:
        copy = pltpu.make_async_remote_copy(
            src_ref=part_ref.at[:, :, :, 1 - me["c"]],
            dst_ref=from_core,
            send_sem=core_sems.at[0],
            recv_sem=core_sems.at[1],
            device_id=device_at(moved(me, size, "c", 1), size),
            device_id_type=MESH,
        )
        copy.start()
        copy.wait()

    def first(i, carry):
        z, x, y = i // (size["x"] * size["y"]), (i // size["y"]) % size["x"], i % size["y"]
        for lo, target in ((0, first_a.at[y, x, z]), (half, first_b.at[x, y, z])):
            total = part_ref[z, x, y, me["c"], :, lo : lo + half].astype(F32)
            if cores == 2:
                total = total + from_core[z, x, y, :, lo : lo + half].astype(F32)
            target[...] = total.astype(BF16)
        return carry

    lax.fori_loop(0, size["x"] * size["y"] * size["z"], first, 0)
    used = [0]

    def exchange(axis, source, landing):
        copies = []
        for d in range(1, size[axis]):
            to = moved(me, size, axis, d)
            copy = pltpu.make_async_remote_copy(
                src_ref=source.at[to[axis]],
                dst_ref=landing.at[size[axis] - d - 1],
                send_sem=sems.at[used[0] + d - 1],
                recv_sem=sems.at[used[0] + 2 * (size[axis] - 1) - d],
                device_id=device_at(to, size),
                device_id_type=MESH,
            )
            copy.start()
            copies.append(copy)
        used[0] += 2 * (size[axis] - 1)
        return copies

    def add(axis, source, landing, target, inner):
        def one(i, carry):
            place = (i // inner, i % inner) if len(target.shape) == 4 else (i,)
            total = source[(me[axis],) + place].astype(F32)
            for d in range(size[axis] - 1):
                total = total + landing[(d,) + place].astype(F32)
            target[place] = total.astype(BF16)
            return carry

        count = 1
        for extent in target.shape[:-2]:
            count *= extent
        lax.fori_loop(0, count, one, 0)

    for copy_a, copy_b in [(exchange("y", first_a, land_a), exchange("x", first_b, land_b))]:
        for copy in copy_a:
            copy.wait()
        add("y", first_a, land_a, second_a, size["z"])
        copy2_a = exchange("x", second_a, land2_a)
        for copy in copy_b:
            copy.wait()
        add("x", first_b, land_b, second_b, size["z"])
        copy2_b = exchange("y", second_b, land2_b)
        for copy in copy2_a:
            copy.wait()
        add("x", second_a, land2_a, third_a, 1)
        copy3_a = exchange("z", third_a, land3_a)
        for copy in copy2_b:
            copy.wait()
        add("y", second_b, land2_b, third_b, 1)
        copy3_b = exchange("z", third_b, land3_b)
        for lo, third, landing, copies in ((0, third_a, land3_a, copy3_a), (half, third_b, land3_b, copy3_b)):
            for copy in copies:
                copy.wait()
            total = third[me["z"]].astype(F32)
            for d in range(size["z"] - 1):
                total = total + landing[d].astype(F32)
            out_ref[:, lo : lo + half] = total


def sum_experts(part, size, collective_id):
    rows, width = part.shape[-2:]
    half = width // 2
    x, y, z = size["x"], size["y"], size["z"]

    def buffer(*lead):
        return pltpu.VMEM(lead + (rows, half), BF16)

    return pl.pallas_call(
        functools.partial(experts_kernel, size),
        out_shape=jax.ShapeDtypeStruct((rows, width), F32),
        in_specs=[pl.BlockSpec(memory_space=pltpu.VMEM)],
        out_specs=pl.BlockSpec(memory_space=pltpu.VMEM),
        scratch_shapes=[
            pltpu.VMEM((z, x, y, rows, width), BF16),
            buffer(y, x, z),
            buffer(x, y, z),
            buffer(y - 1, x, z),
            buffer(x - 1, y, z),
            buffer(x, z),
            buffer(y, z),
            buffer(x - 1, z),
            buffer(y - 1, z),
            buffer(z),
            buffer(z),
            buffer(z - 1),
            buffer(z - 1),
            pltpu.SemaphoreType.DMA((2,)),
            pltpu.SemaphoreType.DMA((4 * (x + y + z - 3),)),
        ],
        compiler_params=pltpu.CompilerParams(
            collective_id=collective_id, has_side_effects=True, vmem_limit_bytes=VMEM_BYTES
        ),
        name="sum_experts",
    )(part)


def lane_tiles(column, lanes):
    return jnp.concatenate([column] * (lanes // column.shape[1]), axis=1)


def end_kernel(delta_ref, drive_ref, input_ref, rate_ref, end_ref):
    rate = -jnp.exp(rate_ref[...])
    lanes = rate.shape[1]

    def step(t, state):
        decay = jnp.exp(delta_ref[pl.ds(t, 1), :] * rate)
        return decay * state + drive_ref[pl.ds(t, 1), :] * lane_tiles(input_ref[t], lanes)

    end_ref[...] = lax.fori_loop(0, delta_ref.shape[0], step, jnp.zeros_like(rate), unroll=8)


def scan_kernel(
    delta_ref, drive_ref, input_ref, output_ref, rate_ref, start_ref, conv_ref, gate_ref, skip_ref, out_ref, y_ref
):
    rate = -jnp.exp(rate_ref[...])
    lanes = rate.shape[1]

    def step(t, state):
        decay = jnp.exp(delta_ref[pl.ds(t, 1), :] * rate)
        state = decay * state + drive_ref[pl.ds(t, 1), :] * lane_tiles(input_ref[t], lanes)
        y_ref[pl.ds(t, 1), :] = jnp.sum(state * lane_tiles(output_ref[t], lanes), axis=0, keepdims=True)
        return state

    lax.fori_loop(0, delta_ref.shape[0], step, start_ref[...], unroll=8)
    scan_out = y_ref[...] + skip_ref[...] * conv_ref[...].astype(F32)
    gate = gate_ref[...].astype(F32)
    out_ref[...] = (scan_out * (gate * jax.nn.sigmoid(gate))).astype(BF16)


def scan_specs(rows, states, lanes):
    wide = pl.BlockSpec((rows, lanes), lambda i: (0, i))
    maps = pl.BlockSpec((rows, states, 128), lambda i: (0, 0, 0))
    state = pl.BlockSpec((states, lanes), lambda i: (0, i))
    return wide, maps, state, pl.BlockSpec((1, lanes), lambda i: (0, i))


def body(
    mixer_input,
    gate_input,
    conv_weight,
    conv_bias,
    rank_weight,
    state_weight,
    delta_weight,
    delta_bias,
    log_rates,
    skip_gain,
    out_proj,
    residual,
    norm_gain,
    router,
    w_gate,
    w_up,
    w_down,
    routes,
):
    seq, exp = lax.axis_size("seq"), lax.axis_size("exp")
    size = axis_sizes(seq, exp)
    taps = conv_weight.shape[0]
    block_rows, width = mixer_input.shape
    route = [(i - 1, i) for i in range(1, seq)]
    rim_rows = lax.ppermute(mixer_input[block_rows - (taps - 1) :], "seq", route)
    padded = jnp.concatenate([rim_rows, mixer_input], axis=0)
    conv_sum = jnp.zeros(mixer_input.shape, F32) + conv_bias[None, :]
    for offset in range(taps):
        conv_sum = conv_sum + conv_weight[offset].astype(F32)[None, :] * padded[
            offset : offset + block_rows
        ].astype(F32)
    conv_act = jax.nn.silu(conv_sum).astype(BF16)
    rank, states = rank_weight.shape[1], log_rates.shape[0]
    narrow = -(-(rank + 2 * states) // 128) * 128
    low_weight = jnp.concatenate(
        [rank_weight, state_weight, jnp.zeros((width, narrow - rank - 2 * states), BF16)], axis=1
    )
    low_part = jnp.dot(conv_act, low_weight, preferred_element_type=F32)
    low = jnp.sum(gather(low_part, size, ("yc",), (), 1), axis=(0, 1))
    delta_low = low[:, :rank].astype(BF16)
    input_map = low[:, rank : rank + states]
    output_map = low[:, rank + states : rank + 2 * states]
    delta = jax.nn.softplus(
        jnp.dot(delta_low, delta_weight, preferred_element_type=F32) + delta_bias[None, :]
    )
    drive = delta * conv_act.astype(F32)
    total_dt = jnp.sum(delta, axis=0)
    input_wide = jnp.broadcast_to(input_map[:, :, None], (block_rows, states, 128))
    output_wide = jnp.broadcast_to(output_map[:, :, None], (block_rows, states, 128))

    lanes = 512 if width % 512 == 0 else 128
    wide, maps, state, line = scan_specs(block_rows, states, lanes)
    last = pl.pallas_call(
        end_kernel,
        grid=(width // lanes,),
        out_shape=jax.ShapeDtypeStruct((states, width), F32),
        in_specs=[wide, wide, maps, state],
        out_specs=state,
        name="block_end",
    )(delta, drive, input_wide, log_rates)
    passing = jnp.concatenate([last, total_dt.reshape(states, width // states)], axis=1).astype(BF16)
    passed = gather(passing, size, ("zx",), (), 2).reshape((seq,) + passing.shape)
    index = lax.axis_index("seq")
    rate = jnp.exp(log_rates)
    start_state = jnp.zeros((states, width), F32)
    for k in range(seq - 1):
        gone = passed[k, :, width:].reshape(1, width).astype(F32)
        following = jnp.exp(-gone * rate) * start_state + passed[k, :, :width].astype(F32)
        start_state = jnp.where(k < index, following, start_state)
    gated = pl.pallas_call(
        scan_kernel,
        grid=(width // lanes,),
        out_shape=jax.ShapeDtypeStruct((block_rows, width), BF16),
        in_specs=[wide, wide, maps, maps, state, state, wide, wide, line],
        out_specs=wide,
        scratch_shapes=[pltpu.VMEM((block_rows, lanes), F32)],
        name="scan",
    )(delta, drive, input_wide, output_wide, log_rates, start_state, conv_act, gate_input, skip_gain[None, :])

    tok_dev, features = residual.shape
    everyone = gather(gated, size, ("zx",), (), 3).reshape(seq * block_rows, width)
    part = jnp.dot(everyone, out_proj, preferred_element_type=F32).astype(BF16)
    part = part.reshape(seq, exp, tok_dev, part.shape[1]).transpose(1, 0, 2, 3)
    hidden = residual.astype(F32) + sum_channels(part, size, 4)
    mean_square = jnp.mean(hidden * hidden, axis=1, keepdims=True)
    normed = (hidden * lax.rsqrt(mean_square + 1e-05) * norm_gain[None, :]).astype(BF16)
    logits = jnp.dot(normed.astype(F32), router, precision=lax.Precision.HIGHEST)
    experts = router.shape[1]
    expert_ids = jnp.arange(experts, dtype=jnp.int32)
    matches = (routes[:, :, None] == expert_ids[None, None, :]).astype(F32)
    chosen = jnp.sum(matches * logits[:, None, :], axis=2)
    route_weights = jax.nn.sigmoid(chosen - chosen[:, ::-1])
    shares = jnp.sum(matches * route_weights[:, :, None], axis=1)
    shares = jnp.pad(shares, ((0, 0), (0, 128 - experts))).astype(BF16)
    rows = gather(
        jnp.concatenate([normed, shares], axis=1), size, ("zxyc", "zyxc"), (features // 2,), 5
    )
    rows = rows.reshape(seq * exp * tok_dev, features + 128)
    own_share = jnp.sum(
        jnp.where(
            jnp.arange(128)[None, :] == lax.axis_index("exp"), rows[:, features:].astype(F32), 0.0
        ),
        axis=1,
        keepdims=True,
    )
    rows = rows[:, :features]
    gate_part = jnp.dot(rows, w_gate[0], preferred_element_type=F32)
    up_part = jnp.dot(rows, w_up[0], preferred_element_type=F32)
    activated = (jax.nn.silu(gate_part) * up_part).astype(BF16)
    part = (jnp.dot(activated, w_down[0], preferred_element_type=F32) * own_share).astype(BF16)
    part = part.reshape(size["z"], size["x"], size["y"], size["c"], tok_dev, features)
    moe_sum = sum_experts(part, size, 6)
    return ((hidden + moe_sum).astype(BF16), moe_sum)


def solution(mesh):
    in_specs = (
        P("seq", "exp"),
        P("seq", "exp"),
        P(None, "exp"),
        P("exp"),
        P("exp", None),
        P("exp", None),
        P(None, "exp"),
        P("exp"),
        P(None, "exp"),
        P("exp"),
        P("exp", "seq"),
        P(("seq", "exp"), None),
        P(),
        P(),
        P("exp", None, "seq"),
        P("exp", None, "seq"),
        P("exp", "seq", None),
        P(("seq", "exp"), None),
    )
    out_specs = (P(("seq", "exp"), None), P(("seq", "exp"), None))
    return jax.shard_map(body, mesh=mesh, in_specs=in_specs, out_specs=out_specs, check_vma=False)
```

time: 637 us -> 252 us (0.40)
  waiting for transfers between devices: 415 us -> 0.01 us
  Pallas kernels: 0 us -> 170 us
  other arithmetic: 97.2 us -> 14.2 us
  blocking collectives: 23 us -> 0 us
  between operations: 14.4 us -> 0.87 us
  local copies, waits for them, and re-layouts: 16.8 us -> 9.1 us
    all_gather x4 -> x0, waiting for transfers between devices: 290 us -> none  [the longest x1 134 us: body(): lax.all_gather(out_proj, 'seq', axis=1, tiled=True)]
    pallas_call x0 -> x8, Pallas kernels: none -> 170 us  [the longest x4 91.8 us: gather(): pl.pallas_call(functools.partial(gather_kernel, size, flows), out_shape=j...]
    reduce_scatter x2 -> x0, waiting for transfers between devices: 109 us -> none  [the longest x1 86 us: body(): lax.psum_scatter(jnp.dot(activated, down_local, preferred_element_type=jn...]
    reduce_sum x66 -> x3, other arithmetic: 70.7 us -> 2.7 us  [the longest x1 1.67 us: body(): low = jnp.sum(gather(low_part, size, ('yc',), (), 1), axis=(0, 1))]
    all_to_all x1 -> x0, waiting for transfers between devices: 13.9 us -> none  [body(): lax.all_to_all(expert_out, 'exp', split_axis=0, concat_axis=0, tiled=True)]
    dynamic_update_slice x64 -> x0, local copies, waits for them, and re-layouts: 13.1 us -> none  [body(): lax.scan(advance, start_state, (decays, driven, output_map))]
    all_to_all x1 -> x0, blocking collectives: 11.9 us -> none  [body(): lax.all_to_all(outbound, 'exp', split_axis=0, concat_axis=0, tiled=True)]
    psum x1 -> x0, blocking collectives: 11.1 us -> none  [body(): delta_sum, state_maps = lax.psum((delta_part, state_part), 'exp')]
  transfers between devices with their start and end apart: 8 -> 1, of which waited for: 8 -> 0; matrix products, arithmetic and copies ran while one was open for 15% -> 1% of each run, Pallas kernels for 0% -> 0%
where the time goes in v1:
time: 252 us; the launch traced here: 251 us
  Pallas kernels  170 us (67%)
  matrix products  51.6 us (20%)
  other arithmetic  14.2 us (6%)
  local copies, waits for them, and re-layouts  9.1 us (4%)
  starting transfers between devices  4.97 us (2%)
    pallas_call x4, Pallas kernels, gather(): pl.pallas_call(functools.partial(gather_kernel, size, flows), out_shape=j...  91.8 us
    pallas_call x1, Pallas kernels, sum_experts(): pl.pallas_call(functools.partial(experts_kernel, size), out_shape=jax.Sha...  45.4 us
    dot_general x1, matrix products, body(): jnp.dot(activated, w_down[0], preferred_element_type=F32) * own_share  28.9 us
    pallas_call x1, Pallas kernels, sum_channels(): pl.pallas_call(functools.partial(channels_kernel, size), out_shape=jax.Sh...  22.3 us
    dot_general x1, matrix products, body(): gate_part = jnp.dot(rows, w_gate[0], preferred_element_type=F32)  14.6 us
    pallas_call x1, Pallas kernels, body(): pl.pallas_call(scan_kernel, grid=(width // lanes,), out_shape=jax.ShapeDt...  6.15 us
  transfers between devices with their start and end apart: 1, of which 0 were waited for; matrix products, arithmetic and copies ran while one was open for 1% of the time, Pallas kernels for 0%

profile of v1, /device:TPU:0, one launch (start us, length us, event | category | flops | bytes accessed | tf_op | source)
XLA Modules:
  0.0 251.0 jit_solution(5007339823610793109)
XLA Ops:
  1.6 5.0 %collective-permute-start = (bf16[3,2048]{1,0:T(4,128)(2,1)S(1)}, bf16[3,2048]{1,0:T(4,128)(2,1)S(1)}, u32[]{:S(2)}, u32[]{:S(2)}) collective-permute-start(bf16[3,2048]{1,0:T(4,128)(2,1)S(1)} %slice.83), channel_id=1, source_target_pairs={{0,4},{4,8},{8,12},{12,16},{16,20},{20,24},{24,28},{1,5},{5,9},{9,... | collective-permute-start | bytes 36872 | tf_op jit(solution)/shard_map/ppermute | solution.py:416
  7.5 1.9 copy.30
  9.5 1.8 multiply_convert_fusion.2.conv_ref
  11.3 2.6 %fusion.19.x_ref = f32[64,384]{1,0:T(8,128)} fusion(bf16[64,2048]{1,0:T(8,128)(2,1)S(1)} %multiply_convert_fusion.2.conv_ref, bf16[2048,32]{1,0:T(8,128)(2,1)} %copy.30, bf16[2048,256]{1,0:T(8,128)(2,1)} %param.22, bf16[384]{0:T(512)(128)(2,1)S(1)} %pad.12.clone), kind=kOutput, calls=%fused_computation.12 | convolution fusion | flops 105381888 | bytes 1540864 | tf_op jit(solution)/shard_map/dot_general | solution.py:429
  13.9 6.7 %gather_yc.1 = f32[2,2,64,384]{3,2,1,0:T(8,128)} custom-call(f32[64,384]{1,0:T(8,128)} %fusion.19.x_ref), custom_call_target="tpu_custom_call" | custom-call | tf_op jit(solution)/shard_map/gather_yc/pallas_call | solution.py:127
  20.6 1.7 reduce_sum.54
  22.3 1.5 fusion.39
  23.8 2.4 fusion.38
  27.2 4.5 %block_end.1 = f32[16,2048]{1,0:T(8,128)} custom-call(f32[64,2048]{1,0:T(8,128)} %get-tuple-element.17.delta_ref, f32[64,2048]{1,0:T(8,128)} %get-tuple-element.10.drive_ref, f32[64,16,128]{2,1,0:T(8,128)} %broadcast_in_dim.19.input_ref, f32[16,2048]{1,0:T(8,128)} %rate_ref.3), custom_call_target="tpu_custom_call" | custom-call | tf_op jit(solution)/shard_map/block_end/pallas_call | solution.py:444
  33.2 16.1 %gather_zx.2 = bf16[4,2,16,2176]{3,2,1,0:T(8,128)(2,1)} custom-call(bf16[16,2176]{1,0:T(8,128)(2,1)} %pad_maximum_fusion.1.x_ref), custom_call_target="tpu_custom_call" | custom-call | tf_op jit(solution)/shard_map/gather_zx/pallas_call | solution.py:127
  50.1 1.9 fusion.29.start_ref
  53.0 6.2 %scan.1.x_ref = bf16[64,2048]{1,0:T(8,128)(2,1)} custom-call(f32[64,2048]{1,0:T(8,128)} %get-tuple-element.17.delta_ref, f32[64,2048]{1,0:T(8,128)} %get-tuple-element.10.drive_ref, f32[64,16,128]{2,1,0:T(8,128)} %broadcast_in_dim.19.input_ref, f32[64,16,128]{2,1,0:T(8,128)} %broadcast_in_dim.20.output_ref, f32[16,2048]{1,0:T(8,128)} %rate_ref.3, ...), custom_call_target="tpu_custom_call" | custom-call | tf_op jit(solution)/shard_map/scan/pallas_call | solution.py:461
  59.2 35.4 %gather_zx.3 = bf16[4,2,64,2048]{3,2,1,0:T(8,128)(2,1)} custom-call(bf16[64,2048]{1,0:T(8,128)(2,1)} %scan.1.x_ref), custom_call_target="tpu_custom_call" | custom-call | tf_op jit(solution)/shard_map/gather_zx/pallas_call | solution.py:127
  94.6 2.9 %convolution_convert_fusion = bf16[512,512]{1,0:T(8,128)(2,1)S(1)} fusion(bf16[512,2048]{1,0:T(8,128)(2,1)} %bitcast.90, bf16[2048,512]{1,0:T(8,128)(2,1)S(1)} %copy-done), kind=kOutput, calls=%fused_computation.18 | convolution fusion | flops 1074003968 | bytes 4718592 | tf_op jit(solution)/shard_map/dot_general | solution.py:473
  98.3 22.3 %sum_channels.1 = f32[16,4096]{1,0:T(8,128)} custom-call(bf16[4,8,16,512]{3,2,1,0:T(8,128)(2,1)} %bitcast.91), custom_call_target="tpu_custom_call" | custom-call | tf_op jit(solution)/shard_map/sum_channels/pallas_call | solution.py:203
  120.7 1.1 multiply_reduce_fusion
  121.8 1.0 multiply_convert_fusion.3
  124.0 33.7 %gather_zxyc.1 = bf16[4,2,2,2,16,4224]{5,4,3,2,1,0:T(8,128)(2,1)} custom-call(bf16[16,4224]{1,0:T(8,128)(2,1)} %fusion.28.x_ref), custom_call_target="tpu_custom_call" | custom-call | tf_op jit(solution)/shard_map/gather_zxyc/pallas_call | solution.py:127
  157.6 1.0 select_reduce_fusion
  158.7 14.6 %fusion.4 = f32[512,1792]{1,0:T(8,128)} fusion(bf16[1,4096,1792]{2,1,0:T(8,128)(2,1)} %param.32, bf16[512,4224]{1,0:T(8,128)(2,1)} %bitcast.87), kind=kOutput, calls=%fused_computation.4 | convolution fusion | flops 7516192768 | bytes 22544384 | tf_op jit(solution)/shard_map/dot_general | solution.py:498
  173.3 28.9 %multiply_convert_fusion = bf16[512,4096]{1,0:T(8,128)(2,1)} fusion(bf16[1,1792,4096]{2,1,0:T(8,128)(2,1)} %param.34, f32[512]{0:T(512)S(1)} %select_reduce_fusion, f32[512,1792]{1,0:T(8,128)} %fusion.4, bf16[1,4096,1792]{2,1,0:T(8,128)(2,1)} %param.33, bf16[512,4224]{1,0:T(8,128)(2,1)} %bitcast.88), kind=kOutput, calls=%fused_computation.6 | convolution fusion | flops 15042084864 | bytes 41420800 | tf_op jit(solution)/shard_map/dot_general | solution.py:501
  202.2 45.4 %sum_experts.1 = f32[16,4096]{1,0:T(8,128)} custom-call(bf16[4,2,2,2,16,4096]{5,4,3,2,1,0:T(8,128)(2,1)} %bitcast.89), custom_call_target="tpu_custom_call" | custom-call | tf_op jit(solution)/shard_map/sum_experts/pallas_call | solution.py:322
  247.7 1.6 add_convert_fusion
  249.3 1.7 copy.36
  (44 shorter events, 8.2 us)
Async XLA Ops:
  0.6 93.9 %copy-start = (bf16[2048,512]{1,0:T(8,128)(2,1)S(1)}, bf16[2048,512]{1,0:T(8,128)(2,1)}, u32[]{:S(2)}) copy-start(bf16[2048,512]{1,0:T(8,128)(2,1)} %param.28) | copy-start | bytes 6291460
  0.6 23.1 %copy-start.10 = (f32[2048]{0:T(1024)S(1)}, f32[2048]{0:T(1024)}, u32[]{:S(2)}) copy-start(f32[2048]{0:T(1024)} %param.25) | copy-start | bytes 24580
  0.7 23.1 %copy-start.6 = (bf16[256,2048]{1,0:T(8,128)(2,1)S(1)}, bf16[256,2048]{1,0:T(8,128)(2,1)}, u32[]{:S(2)}) copy-start(bf16[256,2048]{1,0:T(8,128)(2,1)} %param.24) | copy-start | bytes 3145732
  1.6 7.9 %collective-permute-start = (bf16[3,2048]{1,0:T(4,128)(2,1)S(1)}, bf16[3,2048]{1,0:T(4,128)(2,1)S(1)}, u32[]{:S(2)}, u32[]{:S(2)}) collective-permute-start(bf16[3,2048]{1,0:T(4,128)(2,1)S(1)} %slice.83), channel_id=1, source_target_pairs={{0,4},{4,8},{8,12},{12,16},{16,20},{20,24},{24,28},{1,5},{5,9},{9,... | collective-permute-start | bytes 36872 | tf_op jit(solution)/shard_map/ppermute | solution.py:416
  11.3 15.9 %copy-start.3 = (bf16[64,2048]{1,0:T(8,128)(2,1)}, bf16[64,2048]{1,0:T(8,128)(2,1)S(1)}, u32[]{:S(2)}) copy-start(bf16[64,2048]{1,0:T(8,128)(2,1)S(1)} %multiply_convert_fusion.2.conv_ref) | copy-start | bytes 786436
  13.9 36.2 %copy-start.4 = (f32[16,2048]{1,0:T(8,128)S(1)}, f32[16,2048]{1,0:T(8,128)}, u32[]{:S(2)}) copy-start(f32[16,2048]{1,0:T(8,128)} %rate_ref.3) | copy-start | bytes 393220
  26.2 25.8 %copy-start.7 = (f32[64,16]{1,0:T(8,128)S(1)}, f32[64,16]{1,0:T(8,128)}, u32[]{:S(2)}) copy-start(f32[64,16]{1,0:T(8,128)} %get-tuple-element.11) | copy-start | bytes 12292
  94.5 26.1 %copy-start.5 = (bf16[16,4096]{1,0:T(8,128)(2,1)S(1)}, bf16[16,4096]{1,0:T(8,128)(2,1)}, u32[]{:S(2)}) copy-start(bf16[16,4096]{1,0:T(8,128)(2,1)} %param.29) | copy-start | bytes 393220
  94.6 27.2 %copy-start.9 = (f32[4096]{0:T(1024)S(1)}, f32[4096]{0:T(1024)}, u32[]{:S(2)}) copy-start(f32[4096]{0:T(1024)} %param.30) | copy-start | bytes 49156
  94.6 28.3 %copy-start.8 = (f32[4096,4]{0,1:T(4,128)S(1)}, f32[4096,4]{0,1:T(4,128)}, u32[]{:S(2)}) copy-start(f32[4096,4]{0,1:T(4,128)} %param.31) | copy-start | bytes 196612
  94.6 28.5 %copy-start.11 = (s32[16,2]{0,1:T(2,128)S(1)}, s32[16,2]{0,1:T(2,128)}, u32[]{:S(2)}) copy-start(s32[16,2]{0,1:T(2,128)} %param.35) | copy-start | bytes 388
  173.3 77.7 %copy-start.1 = (bf16[2048,512]{1,0:T(8,128)(2,1)S(1)}, bf16[2048,512]{1,0:T(8,128)(2,1)}, u32[]{:S(2)}) copy-start(bf16[2048,512]{1,0:T(8,128)(2,1)} %param.28) | copy-start | bytes 6291460
  202.2 45.5 %copy-start.2 = (f32[16,4096]{1,0:T(8,128)S(1)}, f32[16,4096]{1,0:T(8,128)}, u32[]{:S(2)}) copy-start(f32[16,4096]{1,0:T(8,128)} %sum_channels.1) | copy-start | bytes 786436

commit v2 on v1

--- a/solution.py
+++ b/solution.py
@@ -84,31 +84,38 @@
             landing = window(out_ref.at[slot(full, path)], lo, hi)
             pltpu.make_async_copy(landing, landing, recv_sem.at[number[(f, full)]]).wait()
 
-    for stage in range(len(flows[0][0])):
-        for offsets in held_after(size, flows[0][0][:stage]):
-            pass
-        lists = [held_after(size, path[:stage]) for path, _, _ in flows]
-        for k in range(max(len(held) for held in lists)):
-            for f, (path, lo, hi) in enumerate(flows):
-                if k >= len(lists[f]):
-                    continue
-                offsets = lists[f][k]
-                arrive(f, offsets)
-                axis = path[stage]
-                for d in range(1, size[axis]):
-                    here = slot(offsets, path)
-                    source = x_ref if not any(offsets) else out_ref.at[here]
-                    lands = offsets + ((size[axis] - d),) + (0,) * (len(path) - stage - 1)
-                    copy = pltpu.make_async_remote_copy(
-                        src_ref=window(source, lo, hi),
-                        dst_ref=window(out_ref.at[here], lo, hi),
-                        send_sem=send_sem.at[len(sends)],
-                        recv_sem=recv_sem.at[number[(f, lands)]],
-                        device_id=device_at(moved(me, size, axis, d), size),
-                        device_id_type=MESH,
-                    )
-                    copy.start()
-                    sends.append(copy)
+    def forward(f, offsets, stage):
+        path, lo, hi = flows[f]
+        here = slot(offsets, path)
+        axis = path[stage]
+        source = x_ref if not any(offsets) else out_ref.at[here]
+        for d in range(1, size[axis]):
+            lands = offsets[:stage] + (size[axis] - d,) + (0,) * (len(path) - stage - 1)
+            copy = pltpu.make_async_remote_copy(
+                src_ref=window(source, lo, hi),
+                dst_ref=window(out_ref.at[here], lo, hi),
+                send_sem=send_sem.at[len(sends)],
+                recv_sem=recv_sem.at[number[(f, lands)]],
+                device_id=device_at(moved(me, size, axis, d), size),
+                device_id_type=MESH,
+            )
+            copy.start()
+            sends.append(copy)
+
+    stages = len(flows[0][0])
+    for stage in range(stages):
+        for f, (path, _, _) in enumerate(flows):
+            forward(f, (0,) * stages, stage)
+    alike = all(path == flows[0][0] for path, _, _ in flows)
+    for came in range(stages):
+        work = []
+        for f, (path, _, _) in enumerate(flows):
+            held = [h for h in held_after(size, path[: came + 1]) if h[came]]
+            work += [(f if alike else k, f, h + (0,) * (stages - came - 1)) for k, h in enumerate(held)]
+        for _, f, offsets in sorted(work, key=lambda item: item[0]):
+            arrive(f, offsets)
+            for stage in range(came + 1, stages):
+                forward(f, offsets, stage)
     for f, (path, _, _) in enumerate(flows):
         for offsets in held_after(size, path):
             arrive(f, offsets)
@@ -224,128 +231,195 @@
 def experts_kernel(size, part_ref, out_ref, *scratch):
     me = own_place(size)
     greet(size, "zxyc")
-    half = part_ref.shape[-1] // 2
-    rows = part_ref.shape[-2]
-    from_core, first_a, first_b, land_a, land_b, second_a, second_b, land2_a, land2_b = scratch[:9]
-    third_a, third_b, land3_a, land3_b, core_sems, sems = scratch[9:]
-    cores = size["c"]
-    pending = []
-    if cores == 2:
-        copy = pltpu.make_async_remote_copy(
-            src_ref=part_ref.at[:, :, :, 1 - me["c"]],
-            dst_ref=from_core,
-            send_sem=core_sems.at[0],
-            recv_sem=core_sems.at[1],
-            device_id=device_at(moved(me, size, "c", 1), size),
-            device_id_type=MESH,
-        )
-        copy.start()
-        copy.wait()
-
-    def first(i, carry):
-        z, x, y = i // (size["x"] * size["y"]), (i // size["y"]) % size["x"], i % size["y"]
-        for lo, target in ((0, first_a.at[y, x, z]), (half, first_b.at[x, y, z])):
-            total = part_ref[z, x, y, me["c"], :, lo : lo + half].astype(F32)
-            if cores == 2:
-                total = total + from_core[z, x, y, :, lo : lo + half].astype(F32)
-            target[...] = total.astype(BF16)
-        return carry
-
-    lax.fori_loop(0, size["x"] * size["y"] * size["z"], first, 0)
-    used = [0]
-
-    def exchange(axis, source, landing):
+    chunks = part_ref.shape[0]
+    width = part_ref.shape[-1]
+    half = width // 2
+    from_core, core_send, core_recv, sems = scratch[:4]
+    flows = (("yxz", scratch[4:9], 0), ("xyz", scratch[9:14], half))
+    hops = sum(size[a] - 1 for a in "xyz")
+
+    def exchange(axis, chunk, flow, before, source, landing):
         copies = []
+        base = (chunk * 2 + flow) * hops + before
         for d in range(1, size[axis]):
             to = moved(me, size, axis, d)
             copy = pltpu.make_async_remote_copy(
-                src_ref=source.at[to[axis]],
-                dst_ref=landing.at[size[axis] - d - 1],
-                send_sem=sems.at[used[0] + d - 1],
-                recv_sem=sems.at[used[0] + 2 * (size[axis] - 1) - d],
+                src_ref=source.at[chunk, to[axis]],
+                dst_ref=landing.at[chunk, size[axis] - d - 1],
+                send_sem=sems.at[0, base + d - 1],
+                recv_sem=sems.at[1, base + size[axis] - d - 1],
                 device_id=device_at(to, size),
                 device_id_type=MESH,
             )
             copy.start()
             copies.append(copy)
-        used[0] += 2 * (size[axis] - 1)
         return copies
 
-    def add(axis, source, landing, target, inner):
-        def one(i, carry):
-            place = (i // inner, i % inner) if len(target.shape) == 4 else (i,)
-            total = source[(me[axis],) + place].astype(F32)
-            for d in range(size[axis] - 1):
-                total = total + landing[(d,) + place].astype(F32)
-            target[place] = total.astype(BF16)
+    core_copies = []
+    if size["c"] == 2:
+        for chunk in range(chunks):
+            copy = pltpu.make_async_remote_copy(
+                src_ref=part_ref.at[chunk, :, :, :, 1 - me["c"]],
+                dst_ref=from_core.at[chunk],
+                send_sem=core_send.at[chunk],
+                recv_sem=core_recv.at[chunk],
+                device_id=device_at(moved(me, size, "c", 1), size),
+                device_id_type=MESH,
+            )
+            copy.start()
+            core_copies.append(copy)
+    flight = {}
+
+    def begin(chunk):
+        if core_copies:
+            core_copies[chunk].wait()
+
+        def first(i, carry):
+            z, x, y = i // (size["x"] * size["y"]), (i // size["y"]) % size["x"], i % size["y"]
+            total = part_ref[chunk, z, x, y, me["c"]].astype(F32)
+            if core_copies:
+                total = total + from_core[chunk, z, x, y].astype(F32)
+            total = total.astype(BF16)
+            flows[0][1][0][chunk, y, x, z] = total[:, :half]
+            flows[1][1][0][chunk, x, y, z] = total[:, half:]
             return carry
 
-        count = 1
-        for extent in target.shape[:-2]:
-            count *= extent
-        lax.fori_loop(0, count, one, 0)
-
-    for copy_a, copy_b in [(exchange("y", first_a, land_a), exchange("x", first_b, land_b))]:
-        for copy in copy_a:
-            copy.wait()
-        add("y", first_a, land_a, second_a, size["z"])
-        copy2_a = exchange("x", second_a, land2_a)
-        for copy in copy_b:
-            copy.wait()
-        add("x", first_b, land_b, second_b, size["z"])
-        copy2_b = exchange("y", second_b, land2_b)
-        for copy in copy2_a:
-            copy.wait()
-        add("x", second_a, land2_a, third_a, 1)
-        copy3_a = exchange("z", third_a, land3_a)
-        for copy in copy2_b:
-            copy.wait()
-        add("y", second_b, land2_b, third_b, 1)
-        copy3_b = exchange("z", third_b, land3_b)
-        for lo, third, landing, copies in ((0, third_a, land3_a, copy3_a), (half, third_b, land3_b, copy3_b)):
-            for copy in copies:
+        lax.fori_loop(0, size["x"] * size["y"] * size["z"], first, 0)
+        for f, (axes, buffers, _) in enumerate(flows):
+            flight[(chunk, f)] = exchange(axes[0], chunk, f, 0, buffers[0], buffers[1])
+
+    def middle(chunk):
+        for f, (axes, buffers, _) in enumerate(flows):
+            for copy in flight[(chunk, f)]:
                 copy.wait()
-            total = third[me["z"]].astype(F32)
+            source, landing, second, landing2, _ = buffers
+            inner = size["z"]
+
+            def one(i, carry, axis=axes[0], source=source, landing=landing, second=second):
+                total = source[chunk, me[axis], i // inner, i % inner].astype(F32)
+                for d in range(size[axis] - 1):
+                    total = total + landing[chunk, d, i // inner, i % inner].astype(F32)
+                second[chunk, i // inner, i % inner] = total.astype(BF16)
+                return carry
+
+            lax.fori_loop(0, size[axes[1]] * inner, one, 0)
+            flight[(chunk, f)] = exchange(axes[1], chunk, f, size[axes[0]] - 1, second, landing2)
+
+    def last(chunk):
+        for f, (axes, buffers, _) in enumerate(flows):
+            for copy in flight[(chunk, f)]:
+                copy.wait()
+            _, _, second, landing2, (third, landing3) = buffers
+
+            def one(i, carry, axis=axes[1], second=second, landing2=landing2, third=third):
+                total = second[chunk, me[axis], i].astype(F32)
+                for d in range(size[axis] - 1):
+                    total = total + landing2[chunk, d, i].astype(F32)
+                third[chunk, i] = total.astype(BF16)
+                return carry
+
+            lax.fori_loop(0, size["z"], one, 0)
+            before = size["x"] + size["y"] - 2
+            flight[(chunk, f)] = exchange("z", chunk, f, before, third, landing3)
+
+    def finish(chunk):
+        for f, (axes, buffers, offset) in enumerate(flows):
+            for copy in flight[(chunk, f)]:
+                copy.wait()
+            third, landing3 = buffers[4]
+            total = third[chunk, me["z"]].astype(F32)
             for d in range(size["z"] - 1):
-                total = total + landing[d].astype(F32)
+                total = total + landing3[chunk, d].astype(F32)
+            lo = chunk * width + offset
             out_ref[:, lo : lo + half] = total
 
+    steps = (begin, middle, last, finish)
+    for tick in range(chunks + len(steps) - 1):
+        for number in reversed(range(len(steps))):
+            if 0 <= tick - number < chunks:
+                steps[number](tick - number)
+
 
 def sum_experts(part, size, collective_id):
-    rows, width = part.shape[-2:]
+    chunks, rows, width = part.shape[0], part.shape[-2], part.shape[-1]
     half = width // 2
     x, y, z = size["x"], size["y"], size["z"]
 
     def buffer(*lead):
-        return pltpu.VMEM(lead + (rows, half), BF16)
+        return pltpu.VMEM((chunks,) + lead + (rows, half), BF16)
+
+    def buffers(a, b):
+        return [buffer(a, b, z), buffer(a - 1, b, z), buffer(b, z), buffer(b - 1, z), buffer(z), buffer(z - 1)]
+
+    hops = 2 * chunks * (x + y + z - 3)
+
+    def kernel(part_ref, out_ref, *scratch):
+        a, b = list(scratch[4:10]), list(scratch[10:16])
+        experts_kernel(
+            size, part_ref, out_ref, *scratch[:4], *a[:4], tuple(a[4:]), *b[:4], tuple(b[4:])
+        )
 
     return pl.pallas_call(
-        functools.partial(experts_kernel, size),
-        out_shape=jax.ShapeDtypeStruct((rows, width), F32),
+        kernel,
+        out_shape=jax.ShapeDtypeStruct((rows, chunks * width), F32),
         in_specs=[pl.BlockSpec(memory_space=pltpu.VMEM)],
         out_specs=pl.BlockSpec(memory_space=pltpu.VMEM),
         scratch_shapes=[
-            pltpu.VMEM((z, x, y, rows, width), BF16),
-            buffer(y, x, z),
-            buffer(x, y, z),
-            buffer(y - 1, x, z),
-            buffer(x - 1, y, z),
-            buffer(x, z),
-            buffer(y, z),
-            buffer(x - 1, z),
-            buffer(y - 1, z),
-            buffer(z),
-            buffer(z),
-            buffer(z - 1),
-            buffer(z - 1),
-            pltpu.SemaphoreType.DMA((2,)),
-            pltpu.SemaphoreType.DMA((4 * (x + y + z - 3),)),
-        ],
+            pltpu.VMEM((chunks, z, x, y, rows, width), BF16),
+            pltpu.SemaphoreType.DMA((chunks,)),
+            pltpu.SemaphoreType.DMA((chunks,)),
+            pltpu.SemaphoreType.DMA((2, hops)),
+        ]
+        + buffers(y, x)
+        + buffers(x, y),
         compiler_params=pltpu.CompilerParams(
             collective_id=collective_id, has_side_effects=True, vmem_limit_bytes=VMEM_BYTES
         ),
         name="sum_experts",
     )(part)
+
+
+def hidden_kernel(rows_ref, gate_ref, up_ref, out_ref):
+    rows = rows_ref[...]
+    gate = jnp.dot(rows, gate_ref[0], preferred_element_type=F32)
+    up = jnp.dot(rows, up_ref[0], preferred_element_type=F32)
+    out_ref[...] = (gate * jax.nn.sigmoid(gate) * up).astype(BF16)
+
+
+def down_kernel(hidden_ref, down_ref, share_ref, out_ref):
+    part = jnp.dot(hidden_ref[...], down_ref[0], preferred_element_type=F32)
+    out_ref[...] = (part * share_ref[...]).astype(BF16)
+
+
+def feed_forward(rows, share, w_gate, w_up, w_down, chunks):
+    count, features, units = rows.shape[0], w_gate.shape[1], w_gate.shape[2]
+    tall = 512 if count % 512 == 0 else count
+    tile = 256 if units % 256 == 0 else units
+    weight = pl.BlockSpec((1, features, tile), lambda n, m: (0, 0, n))
+    params = pltpu.CompilerParams(vmem_limit_bytes=VMEM_BYTES)
+    hidden = pl.pallas_call(
+        hidden_kernel,
+        grid=(units // tile, count // tall),
+        out_shape=jax.ShapeDtypeStruct((count, units), BF16),
+        in_specs=[pl.BlockSpec((tall, features), lambda n, m: (m, 0)), weight, weight],
+        out_specs=pl.BlockSpec((tall, tile), lambda n, m: (m, n)),
+        compiler_params=params,
+        name="hidden_units",
+    )(rows, w_gate, w_up)
+    width = features // chunks
+    return pl.pallas_call(
+        down_kernel,
+        grid=(chunks, count // tall),
+        out_shape=jax.ShapeDtypeStruct((chunks, count, width), BF16),
+        in_specs=[
+            pl.BlockSpec((tall, units), lambda n, m: (m, 0)),
+            pl.BlockSpec((1, units, width), lambda n, m: (0, 0, n)),
+            pl.BlockSpec((tall, 1), lambda n, m: (m, 0)),
+        ],
+        out_specs=pl.BlockSpec((None, tall, width), lambda n, m: (n, m, 0)),
+        compiler_params=params,
+        name="down",
+    )(hidden, w_down, share)
 
 
 def lane_tiles(column, lanes):
@@ -450,7 +524,7 @@
         name="block_end",
     )(delta, drive, input_wide, log_rates)
     passing = jnp.concatenate([last, total_dt.reshape(states, width // states)], axis=1).astype(BF16)
-    passed = gather(passing, size, ("zx",), (), 2).reshape((seq,) + passing.shape)
+    passed = gather(passing, size, ("zx",) * 2, (width // 2,), 2).reshape((seq,) + passing.shape)
     index = lax.axis_index("seq")
     rate = jnp.exp(log_rates)
     start_state = jnp.zeros((states, width), F32)
@@ -469,7 +543,7 @@
     )(delta, drive, input_wide, output_wide, log_rates, start_state, conv_act, gate_input, skip_gain[None, :])
 
     tok_dev, features = residual.shape
-    everyone = gather(gated, size, ("zx",), (), 3).reshape(seq * block_rows, width)
+    everyone = gather(gated, size, ("zx",) * 4, tuple(k * width // 4 for k in range(1, 4)), 3).reshape(seq * block_rows, width)
     part = jnp.dot(everyone, out_proj, preferred_element_type=F32).astype(BF16)
     part = part.reshape(seq, exp, tok_dev, part.shape[1]).transpose(1, 0, 2, 3)
     hidden = residual.astype(F32) + sum_channels(part, size, 4)
@@ -494,12 +568,11 @@
         axis=1,
         keepdims=True,
     )
-    rows = rows[:, :features]
-    gate_part = jnp.dot(rows, w_gate[0], preferred_element_type=F32)
-    up_part = jnp.dot(rows, w_up[0], preferred_element_type=F32)
-    activated = (jax.nn.silu(gate_part) * up_part).astype(BF16)
-    part = (jnp.dot(activated, w_down[0], preferred_element_type=F32) * own_share).astype(BF16)
-    part = part.reshape(size["z"], size["x"], size["y"], size["c"], tok_dev, features)
+    chunks = 4
+    part = feed_forward(rows, own_share, w_gate, w_up, w_down, chunks)
+    part = part.reshape(
+        chunks, size["z"], size["x"], size["y"], size["c"], tok_dev, features // chunks
+    )
     moe_sum = sum_experts(part, size, 6)
     return ((hidden + moe_sum).astype(BF16), moe_sum)
 

time: 252 us -> 220 us (0.87)
  matrix products: 51.6 us -> 7.24 us
  Pallas kernels: 170 us -> 184 us
    dot_general x2 -> x0, matrix products: 43.5 us -> none  [the longest x1 28.9 us: body(): jnp.dot(activated, w_down[0], preferred_element_type=F32) * own_share]
    pallas_call x1 -> x3, Pallas kernels: 45.4 us -> 72.9 us  [the longest x1 39.8 us: sum_experts(): pl.pallas_call(kernel, out_shape=jax.ShapeDtypeStruct((rows, chunks * wid...]
    pallas_call x4, Pallas kernels: 91.8 us -> 84.7 us  [gather(): pl.pallas_call(functools.partial(gather_kernel, size, flows), out_shape=j...]
    pallas_call x1, Pallas kernels: 22.3 us -> 15.9 us  [sum_channels(): pl.pallas_call(functools.partial(channels_kernel, size), out_shape=jax.Sh...]
where the time goes in v2:
time: 220 us; the launch traced here: 219 us
  Pallas kernels  184 us (84%)
  other arithmetic  13.5 us (6%)
  local copies, waits for them, and re-layouts  8.52 us (4%)
  matrix products  7.24 us (3%)
  starting transfers between devices  4.84 us (2%)
    pallas_call x4, Pallas kernels, gather(): pl.pallas_call(functools.partial(gather_kernel, size, flows), out_shape=j...  84.7 us
    pallas_call x1, Pallas kernels, sum_experts(): pl.pallas_call(kernel, out_shape=jax.ShapeDtypeStruct((rows, chunks * wid...  39.8 us
    pallas_call x1, Pallas kernels, feed_forward(): pl.pallas_call(hidden_kernel, grid=(units // tile, count // tall), out_sh...  20.8 us
    pallas_call x1, Pallas kernels, sum_channels(): pl.pallas_call(functools.partial(channels_kernel, size), out_shape=jax.Sh...  15.9 us
    pallas_call x1, Pallas kernels, feed_forward(): pl.pallas_call(down_kernel, grid=(chunks, count // tall), out_shape=jax.S...  12.3 us
    pallas_call x1, Pallas kernels, body(): pl.pallas_call(scan_kernel, grid=(width // lanes,), out_shape=jax.ShapeDt...  6.15 us
    ppermute x1, starting transfers between devices, body(): rim_rows = lax.ppermute(mixer_input[block_rows - (taps - 1):], 'seq', route)  4.84 us
    pallas_call x1, Pallas kernels, body(): pl.pallas_call(end_kernel, grid=(width // lanes,), out_shape=jax.ShapeDty...  4.45 us
  transfers between devices with their start and end apart: 1, of which 0 were waited for; matrix products, arithmetic and copies ran while one was open for 1% of the time, Pallas kernels for 0%

profile of v2, /device:TPU:0, one launch (start us, length us, event | category | flops | bytes accessed | tf_op | source)
XLA Modules:
  0.0 219.2 jit_solution(942135975320772457)
XLA Ops:
  1.6 4.8 %collective-permute-start = (bf16[3,2048]{1,0:T(4,128)(2,1)S(1)}, bf16[3,2048]{1,0:T(4,128)(2,1)S(1)}, u32[]{:S(2)}, u32[]{:S(2)}) collective-permute-start(bf16[3,2048]{1,0:T(4,128)(2,1)S(1)} %slice.80), channel_id=1, source_target_pairs={{0,4},{4,8},{8,12},{12,16},{16,20},{20,24},{24,28},{1,5},{5,9},{9,... | collective-permute-start | bytes 36872 | tf_op jit(solution)/shard_map/ppermute | solution.py:490
  7.4 1.9 copy.32
  9.3 1.8 multiply_convert_fusion.conv_ref
  11.2 2.6 %fusion.x_ref = f32[64,384]{1,0:T(8,128)} fusion(bf16[64,2048]{1,0:T(8,128)(2,1)S(1)} %multiply_convert_fusion.conv_ref, bf16[2048,32]{1,0:T(8,128)(2,1)} %copy.32, bf16[2048,256]{1,0:T(8,128)(2,1)} %param.22, bf16[384]{0:T(512)(128)(2,1)S(1)} %pad.12.clone), kind=kOutput, calls=%fused_computation.1 | convolution fusion | flops 105381888 | bytes 1540864 | tf_op jit(solution)/shard_map/dot_general | solution.py:503
  13.8 6.7 %gather_yc.1 = f32[2,2,64,384]{3,2,1,0:T(8,128)} custom-call(f32[64,384]{1,0:T(8,128)} %fusion.x_ref), custom_call_target="tpu_custom_call" | custom-call | tf_op jit(solution)/shard_map/gather_yc/pallas_call | solution.py:134
  20.5 1.0 reduce_sum.54
  21.6 1.6 fusion.18
  23.2 1.0 broadcast_in_dim.21.input_ref
  24.2 4.4 %block_end.1 = f32[16,2048]{1,0:T(8,128)} custom-call(f32[64,2048]{1,0:T(8,128)} %get-tuple-element.17.delta_ref, f32[64,2048]{1,0:T(8,128)} %get-tuple-element.10.drive_ref, f32[64,16,128]{2,1,0:T(8,128)} %broadcast_in_dim.21.input_ref, f32[16,2048]{1,0:T(8,128)} %rate_ref.3), custom_call_target="tpu_custom_call" | custom-call | tf_op jit(solution)/shard_map/block_end/pallas_call | solution.py:518
  30.1 14.8 %gather_zx.2 = bf16[4,2,16,2176]{3,2,1,0:T(8,128)(2,1)} custom-call(bf16[16,2176]{1,0:T(8,128)(2,1)} %pad_maximum_fusion.1.x_ref), custom_call_target="tpu_custom_call" | custom-call | tf_op jit(solution)/shard_map/gather_zx/pallas_call | solution.py:134
  45.7 1.9 fusion.10.start_ref
  48.6 6.2 %scan.1.x_ref = bf16[64,2048]{1,0:T(8,128)(2,1)} custom-call(f32[64,2048]{1,0:T(8,128)} %get-tuple-element.17.delta_ref, f32[64,2048]{1,0:T(8,128)} %get-tuple-element.10.drive_ref, f32[64,16,128]{2,1,0:T(8,128)} %broadcast_in_dim.21.input_ref, f32[64,16,128]{2,1,0:T(8,128)} %broadcast_in_dim.22.output_ref, f32[16,2048]{1,0:T(8,128)} %rate_ref.3, ...), custom_call_target="tpu_custom_call" | custom-call | tf_op jit(solution)/shard_map/scan/pallas_call | solution.py:535
  54.7 32.6 %gather_zx.3 = bf16[4,2,64,2048]{3,2,1,0:T(8,128)(2,1)} custom-call(bf16[64,2048]{1,0:T(8,128)(2,1)} %scan.1.x_ref), custom_call_target="tpu_custom_call" | custom-call | tf_op jit(solution)/shard_map/gather_zx/pallas_call | solution.py:134
  87.4 2.9 %convolution_convert_fusion = bf16[512,512]{1,0:T(8,128)(2,1)S(1)} fusion(bf16[512,2048]{1,0:T(8,128)(2,1)} %bitcast.75, bf16[2048,512]{1,0:T(8,128)(2,1)S(1)} %copy-done), kind=kOutput, calls=%fused_computation.7 | convolution fusion | flops 1074003968 | bytes 4718592 | tf_op jit(solution)/shard_map/dot_general | solution.py:547
  91.1 15.9 %sum_channels.1 = f32[16,4096]{1,0:T(8,128)} custom-call(bf16[4,8,16,512]{3,2,1,0:T(8,128)(2,1)} %bitcast.76), custom_call_target="tpu_custom_call" | custom-call | tf_op jit(solution)/shard_map/sum_channels/pallas_call | solution.py:210
  107.0 1.1 multiply_reduce_fusion
  108.1 1.0 multiply_convert_fusion.1
  110.3 30.7 %gather_zxyc.1 = bf16[4,2,2,2,16,4224]{5,4,3,2,1,0:T(8,128)(2,1)} custom-call(bf16[16,4224]{1,0:T(8,128)(2,1)} %fusion.9.x_ref), custom_call_target="tpu_custom_call" | custom-call | tf_op jit(solution)/shard_map/gather_zxyc/pallas_call | solution.py:134
  141.0 1.0 select_reduce_fusion
  142.9 20.8 %hidden_units.1.hidden_ref = bf16[512,1792]{1,0:T(8,128)(2,1)} custom-call(bf16[512,4224]{1,0:T(8,128)(2,1)} %bitcast.73, bf16[1,4096,1792]{2,1,0:T(8,128)(2,1)} %gate_ref.3, bf16[1,4096,1792]{2,1,0:T(8,128)(2,1)} %up_ref.1), custom_call_target="tpu_custom_call" | custom-call | tf_op jit(solution)/shard_map/hidden_units/pallas_call | solution.py:400
  163.7 12.3 %down.1 = bf16[4,512,1024]{2,1,0:T(8,128)(2,1)} custom-call(bf16[512,1792]{1,0:T(8,128)(2,1)} %hidden_units.1.hidden_ref, bf16[1,1792,4096]{2,1,0:T(8,128)(2,1)} %down_ref.1, f32[512,1]{1,0:T(8,128)} %copy.35.share_ref), custom_call_target="tpu_custom_call" | custom-call | tf_op jit(solution)/shard_map/down/pallas_call | solution.py:410
  176.0 39.8 %sum_experts.1 = f32[16,4096]{1,0:T(8,128)} custom-call(bf16[4,4,2,2,2,16,1024]{6,5,4,3,2,1,0:T(8,128)(2,1)} %bitcast.74), custom_call_target="tpu_custom_call" | custom-call | tf_op jit(solution)/shard_map/sum_experts/pallas_call | solution.py:362
  215.8 1.6 add_convert_fusion
  217.5 1.7 copy.39
  (43 shorter events, 8.1 us)
Async XLA Ops:
  0.6 86.7 %copy-start = (bf16[2048,512]{1,0:T(8,128)(2,1)S(1)}, bf16[2048,512]{1,0:T(8,128)(2,1)}, u32[]{:S(2)}) copy-start(bf16[2048,512]{1,0:T(8,128)(2,1)} %param.28) | copy-start | bytes 6291460
  1.6 7.8 %collective-permute-start = (bf16[3,2048]{1,0:T(4,128)(2,1)S(1)}, bf16[3,2048]{1,0:T(4,128)(2,1)S(1)}, u32[]{:S(2)}, u32[]{:S(2)}) collective-permute-start(bf16[3,2048]{1,0:T(4,128)(2,1)S(1)} %slice.80), channel_id=1, source_target_pairs={{0,4},{4,8},{8,12},{12,16},{16,20},{20,24},{24,28},{1,5},{5,9},{9,... | collective-permute-start | bytes 36872 | tf_op jit(solution)/shard_map/ppermute | solution.py:490
  11.2 10.4 %copy-start.3 = (bf16[64,2048]{1,0:T(8,128)(2,1)}, bf16[64,2048]{1,0:T(8,128)(2,1)S(1)}, u32[]{:S(2)}) copy-start(bf16[64,2048]{1,0:T(8,128)(2,1)S(1)} %multiply_convert_fusion.conv_ref) | copy-start | bytes 786436
  11.2 10.4 %copy-start.6 = (bf16[256,2048]{1,0:T(8,128)(2,1)S(1)}, bf16[256,2048]{1,0:T(8,128)(2,1)}, u32[]{:S(2)}) copy-start(bf16[256,2048]{1,0:T(8,128)(2,1)} %param.24) | copy-start | bytes 3145732
  11.2 10.4 %copy-start.9 = (f32[2048]{0:T(1024)S(1)}, f32[2048]{0:T(1024)}, u32[]{:S(2)}) copy-start(f32[2048]{0:T(1024)} %param.25) | copy-start | bytes 24580
  23.1 22.5 %copy-start.4 = (f32[16,2048]{1,0:T(8,128)S(1)}, f32[16,2048]{1,0:T(8,128)}, u32[]{:S(2)}) copy-start(f32[16,2048]{1,0:T(8,128)} %rate_ref.3) | copy-start | bytes 393220
  87.3 19.6 %copy-start.5 = (bf16[16,4096]{1,0:T(8,128)(2,1)S(1)}, bf16[16,4096]{1,0:T(8,128)(2,1)}, u32[]{:S(2)}) copy-start(bf16[16,4096]{1,0:T(8,128)(2,1)} %param.29) | copy-start | bytes 393220
  90.2 17.9 %copy-start.8 = (f32[4096]{0:T(1024)S(1)}, f32[4096]{0:T(1024)}, u32[]{:S(2)}) copy-start(f32[4096]{0:T(1024)} %param.30) | copy-start | bytes 49156
  90.2 18.9 %copy-start.7 = (f32[4096,4]{0,1:T(4,128)S(1)}, f32[4096,4]{0,1:T(4,128)}, u32[]{:S(2)}) copy-start(f32[4096,4]{0,1:T(4,128)} %param.31) | copy-start | bytes 196612
  90.3 19.1 %copy-start.10 = (s32[16,2]{0,1:T(2,128)S(1)}, s32[16,2]{0,1:T(2,128)}, u32[]{:S(2)}) copy-start(s32[16,2]{0,1:T(2,128)} %param.35) | copy-start | bytes 388
  176.0 43.1 %copy-start.1 = (bf16[2048,512]{1,0:T(8,128)(2,1)S(1)}, bf16[2048,512]{1,0:T(8,128)(2,1)}, u32[]{:S(2)}) copy-start(bf16[2048,512]{1,0:T(8,128)(2,1)} %param.28) | copy-start | bytes 6291460
  176.0 39.8 %copy-start.2 = (f32[16,4096]{1,0:T(8,128)S(1)}, f32[16,4096]{1,0:T(8,128)}, u32[]{:S(2)}) copy-start(f32[16,4096]{1,0:T(8,128)} %sum_channels.1) | copy-start | bytes 786436

commit v3 on v2

--- a/solution.py
+++ b/solution.py
@@ -228,8 +228,16 @@
     )(part)
 
 
-def experts_kernel(size, part_ref, out_ref, *scratch):
+def experts_kernel(size, hidden_ref, share_ref, down_ref, out_ref, weight, weight_sem, part_ref, *scratch):
     me = own_place(size)
+    fetches = []
+    for chunk in range(part_ref.shape[0]):
+        wide = part_ref.shape[-1]
+        fetch = pltpu.make_async_copy(
+            down_ref.at[0, :, chunk * wide : (chunk + 1) * wide], weight.at[chunk], weight_sem.at[chunk]
+        )
+        fetch.start()
+        fetches.append(fetch)
     greet(size, "zxyc")
     chunks = part_ref.shape[0]
     width = part_ref.shape[-1]
@@ -256,8 +264,31 @@
         return copies
 
     core_copies = []
-    if size["c"] == 2:
-        for chunk in range(chunks):
+    lead = part_ref.shape[2:-1]
+    per_plane = 1
+    for extent in lead:
+        per_plane *= extent
+
+    def multiply(chunk):
+        fetches[chunk].wait()
+
+        def plane(k, carry):
+            rows = pl.ds(k * per_plane, per_plane)
+            product = jnp.dot(hidden_ref[rows, :], weight[chunk], preferred_element_type=F32)
+            product = (product * share_ref[rows, :]).astype(BF16)
+            part_ref[chunk, k] = product.reshape(lead + (width,))
+            return carry
+
+        def whole():
+            product = jnp.dot(hidden_ref[...], weight[chunk], preferred_element_type=F32)
+            product = (product * share_ref[...]).astype(BF16)
+            part_ref[chunk] = product.reshape((size["z"],) + lead + (width,))
+
+        if hidden_ref.shape[0] <= 512:
+            whole()
+        else:
+            lax.fori_loop(0, size["z"], plane, 0)
+        if size["c"] == 2:
             copy = pltpu.make_async_remote_copy(
                 src_ref=part_ref.at[chunk, :, :, :, 1 - me["c"]],
                 dst_ref=from_core.at[chunk],
@@ -333,15 +364,16 @@
             lo = chunk * width + offset
             out_ref[:, lo : lo + half] = total
 
-    steps = (begin, middle, last, finish)
+    steps = (multiply, begin, middle, last, finish)
     for tick in range(chunks + len(steps) - 1):
-        for number in reversed(range(len(steps))):
+        for number in (0, 4, 3, 2, 1):
             if 0 <= tick - number < chunks:
                 steps[number](tick - number)
 
 
-def sum_experts(part, size, collective_id):
-    chunks, rows, width = part.shape[0], part.shape[-2], part.shape[-1]
+def sum_experts(hidden, share, w_down, size, rows, chunks, collective_id):
+    units, features = w_down.shape[1:]
+    width = features // chunks
     half = width // 2
     x, y, z = size["x"], size["y"], size["z"]
 
@@ -353,18 +385,26 @@
 
     hops = 2 * chunks * (x + y + z - 3)
 
-    def kernel(part_ref, out_ref, *scratch):
+    def kernel(hidden_ref, share_ref, down_ref, out_ref, weight, weight_sem, part_ref, *scratch):
         a, b = list(scratch[4:10]), list(scratch[10:16])
         experts_kernel(
-            size, part_ref, out_ref, *scratch[:4], *a[:4], tuple(a[4:]), *b[:4], tuple(b[4:])
+            size, hidden_ref, share_ref, down_ref, out_ref, weight, weight_sem, part_ref,
+            *scratch[:4], *a[:4], tuple(a[4:]), *b[:4], tuple(b[4:])
         )
 
     return pl.pallas_call(
         kernel,
         out_shape=jax.ShapeDtypeStruct((rows, chunks * width), F32),
-        in_specs=[pl.BlockSpec(memory_space=pltpu.VMEM)],
+        in_specs=[
+            pl.BlockSpec(memory_space=pltpu.VMEM),
+            pl.BlockSpec(memory_space=pltpu.VMEM),
+            pl.BlockSpec(memory_space=pl.ANY),
+        ],
         out_specs=pl.BlockSpec(memory_space=pltpu.VMEM),
         scratch_shapes=[
+            pltpu.VMEM((chunks, units, width), BF16),
+            pltpu.SemaphoreType.DMA((chunks,)),
+            pltpu.VMEM((chunks, z, x, y, size["c"], rows, width), BF16),
             pltpu.VMEM((chunks, z, x, y, rows, width), BF16),
             pltpu.SemaphoreType.DMA((chunks,)),
             pltpu.SemaphoreType.DMA((chunks,)),
@@ -376,7 +416,7 @@
             collective_id=collective_id, has_side_effects=True, vmem_limit_bytes=VMEM_BYTES
         ),
         name="sum_experts",
-    )(part)
+    )(hidden, share, w_down)
 
 
 def hidden_kernel(rows_ref, gate_ref, up_ref, out_ref):
@@ -386,18 +426,13 @@
     out_ref[...] = (gate * jax.nn.sigmoid(gate) * up).astype(BF16)
 
 
-def down_kernel(hidden_ref, down_ref, share_ref, out_ref):
-    part = jnp.dot(hidden_ref[...], down_ref[0], preferred_element_type=F32)
-    out_ref[...] = (part * share_ref[...]).astype(BF16)
-
-
-def feed_forward(rows, share, w_gate, w_up, w_down, chunks):
+def hidden_units(rows, w_gate, w_up):
     count, features, units = rows.shape[0], w_gate.shape[1], w_gate.shape[2]
     tall = 512 if count % 512 == 0 else count
     tile = 256 if units % 256 == 0 else units
     weight = pl.BlockSpec((1, features, tile), lambda n, m: (0, 0, n))
     params = pltpu.CompilerParams(vmem_limit_bytes=VMEM_BYTES)
-    hidden = pl.pallas_call(
+    return pl.pallas_call(
         hidden_kernel,
         grid=(units // tile, count // tall),
         out_shape=jax.ShapeDtypeStruct((count, units), BF16),
@@ -406,20 +441,6 @@
         compiler_params=params,
         name="hidden_units",
     )(rows, w_gate, w_up)
-    width = features // chunks
-    return pl.pallas_call(
-        down_kernel,
-        grid=(chunks, count // tall),
-        out_shape=jax.ShapeDtypeStruct((chunks, count, width), BF16),
-        in_specs=[
-            pl.BlockSpec((tall, units), lambda n, m: (m, 0)),
-            pl.BlockSpec((1, units, width), lambda n, m: (0, 0, n)),
-            pl.BlockSpec((tall, 1), lambda n, m: (m, 0)),
-        ],
-        out_specs=pl.BlockSpec((None, tall, width), lambda n, m: (n, m, 0)),
-        compiler_params=params,
-        name="down",
-    )(hidden, w_down, share)
 
 
 def lane_tiles(column, lanes):
@@ -568,12 +589,8 @@
         axis=1,
         keepdims=True,
     )
-    chunks = 4
-    part = feed_forward(rows, own_share, w_gate, w_up, w_down, chunks)
-    part = part.reshape(
-        chunks, size["z"], size["x"], size["y"], size["c"], tok_dev, features // chunks
-    )
-    moe_sum = sum_experts(part, size, 6)
+    activated = hidden_units(rows, w_gate, w_up)
+    moe_sum = sum_experts(activated, own_share, w_down, size, tok_dev, 4, 6)
     return ((hidden + moe_sum).astype(BF16), moe_sum)
 
 

time: 220 us -> 210 us (0.955)
  Pallas kernels: 184 us -> 174 us
    pallas_call x2 -> x1, Pallas kernels: 33.1 us -> 20.8 us  [hidden_units(): pl.pallas_call(hidden_kernel, grid=(units // tile, count // tall), out_sh...]
    pallas_call x1, Pallas kernels: 39.8 us -> 42.2 us  [sum_experts(): pl.pallas_call(kernel, out_shape=jax.ShapeDtypeStruct((rows, chunks * wid...]
where the time goes in v3:
time: 210 us; the launch traced here: 209 us
  Pallas kernels  174 us (83%)
  other arithmetic  13.5 us (6%)
  local copies, waits for them, and re-layouts  8.51 us (4%)
  matrix products  7.24 us (3%)
  starting transfers between devices  4.84 us (2%)
    pallas_call x4, Pallas kernels, gather(): pl.pallas_call(functools.partial(gather_kernel, size, flows), out_shape=j...  84.7 us
    pallas_call x1, Pallas kernels, sum_experts(): pl.pallas_call(kernel, out_shape=jax.ShapeDtypeStruct((rows, chunks * wid...  42.2 us
    pallas_call x1, Pallas kernels, hidden_units(): pl.pallas_call(hidden_kernel, grid=(units // tile, count // tall), out_sh...  20.8 us
    pallas_call x1, Pallas kernels, sum_channels(): pl.pallas_call(functools.partial(channels_kernel, size), out_shape=jax.Sh...  15.9 us
    pallas_call x1, Pallas kernels, body(): pl.pallas_call(scan_kernel, grid=(width // lanes,), out_shape=jax.ShapeDt...  6.15 us
    ppermute x1, starting transfers between devices, body(): rim_rows = lax.ppermute(mixer_input[block_rows - (taps - 1):], 'seq', route)  4.84 us
    pallas_call x1, Pallas kernels, body(): pl.pallas_call(end_kernel, grid=(width // lanes,), out_shape=jax.ShapeDty...  4.45 us
  transfers between devices with their start and end apart: 1, of which 0 were waited for; matrix products, arithmetic and copies ran while one was open for 1% of the time, Pallas kernels for 0%

profile of v3, /device:TPU:0, one launch (start us, length us, event | category | flops | bytes accessed | tf_op | source)
XLA Modules:
  0.0 209.2 jit_solution(2252998185773928748)
XLA Ops:
  1.6 4.8 %collective-permute-start = (bf16[3,2048]{1,0:T(4,128)(2,1)S(1)}, bf16[3,2048]{1,0:T(4,128)(2,1)S(1)}, u32[]{:S(2)}, u32[]{:S(2)}) collective-permute-start(bf16[3,2048]{1,0:T(4,128)(2,1)S(1)} %slice.80), channel_id=1, source_target_pairs={{0,4},{4,8},{8,12},{12,16},{16,20},{20,24},{24,28},{1,5},{5,9},{9,... | collective-permute-start | bytes 36872 | tf_op jit(solution)/shard_map/ppermute | solution.py:511
  7.4 1.9 copy.32
  9.3 1.8 multiply_convert_fusion.conv_ref
  11.2 2.6 %fusion.x_ref = f32[64,384]{1,0:T(8,128)} fusion(bf16[64,2048]{1,0:T(8,128)(2,1)S(1)} %multiply_convert_fusion.conv_ref, bf16[2048,32]{1,0:T(8,128)(2,1)} %copy.32, bf16[2048,256]{1,0:T(8,128)(2,1)} %param.22, bf16[384]{0:T(512)(128)(2,1)S(1)} %pad.12.clone), kind=kOutput, calls=%fused_computation.1 | convolution fusion | flops 105381888 | bytes 1540864 | tf_op jit(solution)/shard_map/dot_general | solution.py:524
  13.8 6.7 %gather_yc.1 = f32[2,2,64,384]{3,2,1,0:T(8,128)} custom-call(f32[64,384]{1,0:T(8,128)} %fusion.x_ref), custom_call_target="tpu_custom_call" | custom-call | tf_op jit(solution)/shard_map/gather_yc/pallas_call | solution.py:134
  20.5 1.0 reduce_sum.54
  21.6 1.6 fusion.18
  23.2 1.0 broadcast_in_dim.21.input_ref
  24.2 4.4 %block_end.1 = f32[16,2048]{1,0:T(8,128)} custom-call(f32[64,2048]{1,0:T(8,128)} %get-tuple-element.17.delta_ref, f32[64,2048]{1,0:T(8,128)} %get-tuple-element.10.drive_ref, f32[64,16,128]{2,1,0:T(8,128)} %broadcast_in_dim.21.input_ref, f32[16,2048]{1,0:T(8,128)} %rate_ref.3), custom_call_target="tpu_custom_call" | custom-call | tf_op jit(solution)/shard_map/block_end/pallas_call | solution.py:539
  30.1 14.8 %gather_zx.2 = bf16[4,2,16,2176]{3,2,1,0:T(8,128)(2,1)} custom-call(bf16[16,2176]{1,0:T(8,128)(2,1)} %pad_maximum_fusion.1.x_ref), custom_call_target="tpu_custom_call" | custom-call | tf_op jit(solution)/shard_map/gather_zx/pallas_call | solution.py:134
  45.7 1.9 fusion.10.start_ref
  47.6 1.0 broadcast_in_dim.22.output_ref
  48.6 6.2 %scan.1.x_ref = bf16[64,2048]{1,0:T(8,128)(2,1)} custom-call(f32[64,2048]{1,0:T(8,128)} %get-tuple-element.17.delta_ref, f32[64,2048]{1,0:T(8,128)} %get-tuple-element.10.drive_ref, f32[64,16,128]{2,1,0:T(8,128)} %broadcast_in_dim.21.input_ref, f32[64,16,128]{2,1,0:T(8,128)} %broadcast_in_dim.22.output_ref, f32[16,2048]{1,0:T(8,128)} %rate_ref.3, ...), custom_call_target="tpu_custom_call" | custom-call | tf_op jit(solution)/shard_map/scan/pallas_call | solution.py:556
  54.7 32.6 %gather_zx.3 = bf16[4,2,64,2048]{3,2,1,0:T(8,128)(2,1)} custom-call(bf16[64,2048]{1,0:T(8,128)(2,1)} %scan.1.x_ref), custom_call_target="tpu_custom_call" | custom-call | tf_op jit(solution)/shard_map/gather_zx/pallas_call | solution.py:134
  87.4 2.9 %convolution_convert_fusion = bf16[512,512]{1,0:T(8,128)(2,1)S(1)} fusion(bf16[512,2048]{1,0:T(8,128)(2,1)} %bitcast.73, bf16[2048,512]{1,0:T(8,128)(2,1)S(1)} %copy-done), kind=kOutput, calls=%fused_computation.7 | convolution fusion | flops 1074003968 | bytes 4718592 | tf_op jit(solution)/shard_map/dot_general | solution.py:568
  91.1 15.9 %sum_channels.1 = f32[16,4096]{1,0:T(8,128)} custom-call(bf16[4,8,16,512]{3,2,1,0:T(8,128)(2,1)} %bitcast.74), custom_call_target="tpu_custom_call" | custom-call | tf_op jit(solution)/shard_map/sum_channels/pallas_call | solution.py:210
  107.0 1.1 multiply_reduce_fusion
  108.1 1.0 multiply_convert_fusion.1
  110.3 30.7 %gather_zxyc.1 = bf16[4,2,2,2,16,4224]{5,4,3,2,1,0:T(8,128)(2,1)} custom-call(bf16[16,4224]{1,0:T(8,128)(2,1)} %fusion.9.x_ref), custom_call_target="tpu_custom_call" | custom-call | tf_op jit(solution)/shard_map/gather_zxyc/pallas_call | solution.py:134
  141.0 1.0 select_reduce_fusion
  142.9 20.8 %hidden_units.1.hidden_ref = bf16[512,1792]{1,0:T(8,128)(2,1)} custom-call(bf16[512,4224]{1,0:T(8,128)(2,1)} %bitcast.72, bf16[1,4096,1792]{2,1,0:T(8,128)(2,1)} %gate_ref.3, bf16[1,4096,1792]{2,1,0:T(8,128)(2,1)} %up_ref.1), custom_call_target="tpu_custom_call" | custom-call | tf_op jit(solution)/shard_map/hidden_units/pallas_call | solution.py:435
  163.7 42.2 %sum_experts.1 = f32[16,4096]{1,0:T(8,128)} custom-call(bf16[512,1792]{1,0:T(8,128)(2,1)} %hidden_units.1.hidden_ref, f32[512,1]{1,0:T(8,128)} %copy.35.share_ref, bf16[1,1792,4096]{2,1,0:T(8,128)(2,1)} %down_ref.1), custom_call_target="tpu_custom_call" | custom-call | tf_op jit(solution)/shard_map/sum_experts/pallas_call | solution.py:395
  205.9 1.6 add_convert_fusion
  207.5 1.7 copy.39
  (40 shorter events, 7.1 us)
Async XLA Ops:
  0.6 86.7 %copy-start = (bf16[2048,512]{1,0:T(8,128)(2,1)S(1)}, bf16[2048,512]{1,0:T(8,128)(2,1)}, u32[]{:S(2)}) copy-start(bf16[2048,512]{1,0:T(8,128)(2,1)} %param.28) | copy-start | bytes 6291460
  1.6 7.8 %collective-permute-start = (bf16[3,2048]{1,0:T(4,128)(2,1)S(1)}, bf16[3,2048]{1,0:T(4,128)(2,1)S(1)}, u32[]{:S(2)}, u32[]{:S(2)}) collective-permute-start(bf16[3,2048]{1,0:T(4,128)(2,1)S(1)} %slice.80), channel_id=1, source_target_pairs={{0,4},{4,8},{8,12},{12,16},{16,20},{20,24},{24,28},{1,5},{5,9},{9,... | collective-permute-start | bytes 36872 | tf_op jit(solution)/shard_map/ppermute | solution.py:511
  11.2 10.4 %copy-start.2 = (bf16[64,2048]{1,0:T(8,128)(2,1)}, bf16[64,2048]{1,0:T(8,128)(2,1)S(1)}, u32[]{:S(2)}) copy-start(bf16[64,2048]{1,0:T(8,128)(2,1)S(1)} %multiply_convert_fusion.conv_ref) | copy-start | bytes 786436
  11.2 10.4 %copy-start.5 = (bf16[256,2048]{1,0:T(8,128)(2,1)S(1)}, bf16[256,2048]{1,0:T(8,128)(2,1)}, u32[]{:S(2)}) copy-start(bf16[256,2048]{1,0:T(8,128)(2,1)} %param.24) | copy-start | bytes 3145732
  11.2 10.4 %copy-start.8 = (f32[2048]{0:T(1024)S(1)}, f32[2048]{0:T(1024)}, u32[]{:S(2)}) copy-start(f32[2048]{0:T(1024)} %param.25) | copy-start | bytes 24580
  23.1 22.5 %copy-start.3 = (f32[16,2048]{1,0:T(8,128)S(1)}, f32[16,2048]{1,0:T(8,128)}, u32[]{:S(2)}) copy-start(f32[16,2048]{1,0:T(8,128)} %rate_ref.3) | copy-start | bytes 393220
  87.3 19.6 %copy-start.4 = (bf16[16,4096]{1,0:T(8,128)(2,1)S(1)}, bf16[16,4096]{1,0:T(8,128)(2,1)}, u32[]{:S(2)}) copy-start(bf16[16,4096]{1,0:T(8,128)(2,1)} %param.29) | copy-start | bytes 393220
  90.2 17.9 %copy-start.7 = (f32[4096]{0:T(1024)S(1)}, f32[4096]{0:T(1024)}, u32[]{:S(2)}) copy-start(f32[4096]{0:T(1024)} %param.30) | copy-start | bytes 49156
  90.2 18.9 %copy-start.6 = (f32[4096,4]{0,1:T(4,128)S(1)}, f32[4096,4]{0,1:T(4,128)}, u32[]{:S(2)}) copy-start(f32[4096,4]{0,1:T(4,128)} %param.31) | copy-start | bytes 196612
  90.3 19.1 %copy-start.9 = (s32[16,2]{0,1:T(2,128)S(1)}, s32[16,2]{0,1:T(2,128)}, u32[]{:S(2)}) copy-start(s32[16,2]{0,1:T(2,128)} %param.35) | copy-start | bytes 388
  163.7 42.2 %copy-start.1 = (f32[16,4096]{1,0:T(8,128)S(1)}, f32[16,4096]{1,0:T(8,128)}, u32[]{:S(2)}) copy-start(f32[16,4096]{1,0:T(8,128)} %sum_channels.1) | copy-start | bytes 786436
